TPU v7x, 32 devices: a whole 2x2x4 slice. The times are simulated.
32 devices in a mesh: section: 4 (over x, core), dp: 2 (over y), expert: 4 (over z).
Axes of the slice: x: 2, y: 2, z: 4, core: 2. Of those that a mesh axis runs over, the one named last changes fastest.
Arguments:
- incoming: bfloat16 [4, 2, 128, 3584], P('section', None, ('dp', 'expert')), may hold values from -6 to 6
- stash: bfloat16 [4, 2, 128, 3584], P('section', None, ('dp', 'expert')), may hold values from -6 to 6
- expert_ids: int32 [4, 2, 128, 2], P('section', None, ('dp', 'expert')), may hold values from 0 to 3, all different within a row; in each aligned block of 16 rows (0 to 15, 16 to 31, ..., all dimensions but the last counted through in order) at most 12 rows name the same one
- route_weight: float32 [4, 2, 128, 2], P('section', None, ('dp', 'expert')), may hold values from 0.1 to 1
- w_gate: bfloat16 [4, 4, 3584, 2048], P('section', 'expert', None, 'dp'), may hold values from -0.09375 to 0.09375
- w_up: bfloat16 [4, 4, 3584, 2048], P('section', 'expert', None, 'dp'), may hold values from -0.09375 to 0.09375
- w_down: bfloat16 [4, 4, 2048, 3584], P('section', 'expert', 'dp'), may hold values from -0.125 to 0.125
Outputs:
- input_grad: bfloat16 [4, 2, 128, 3584], P('section', None, ('dp', 'expert'))
- grad_gate: bfloat16 [4, 4, 3584, 2048], P('section', 'expert', None, 'dp')
- grad_up: bfloat16 [4, 4, 3584, 2048], P('section', 'expert', None, 'dp')
- grad_down: bfloat16 [4, 4, 2048, 3584], P('section', 'expert', 'dp')
Inputs may be any that keep to these rules, and one draw needn't show every extreme that they name: `expert_ids`: each token names 2 different experts. Among the 16 tokens of one device in one micro-batch (aligned blocks of rows), no expert is named by more than 12 of them, a bound that some block reaches.
All inputs are finite; a program needn't handle non-finite values.
Results may differ from a plain program's by a relative error of at most 0.01.
Values may be sent and summed in bfloat16 or wider, within the bound.
A program may use at most 128 MiB of HBM per device.

v0:
```python
import jax
import jax.numpy as jnp
from jax import lax
from jax.sharding import PartitionSpec as P


def passed_along(x, axis, by):
    length = lax.axis_size(axis)
    return lax.ppermute(x, axis, [(i, (i + by) % length) for i in range(length)])


def slice_backward(pair_inputs, pair_scaled, gate_slice, up_slice, down_slice):
    contract_rows = (((0,), (0,)), ((), ()))
    contract_last = (((1,), (1,)), ((), ()))
    gate_pre = jnp.dot(pair_inputs, gate_slice, preferred_element_type=jnp.float32)
    up_pre = jnp.dot(pair_inputs, up_slice, preferred_element_type=jnp.float32)
    logistic = jax.nn.sigmoid(gate_pre)
    activated = gate_pre * logistic
    hidden = (activated * up_pre).astype(jnp.bfloat16)
    hidden_grad = lax.dot_general(
        pair_scaled, down_slice, contract_last, preferred_element_type=jnp.float32
    )
    gate_grad = (hidden_grad * up_pre * logistic * (1.0 + gate_pre * (1.0 - logistic))).astype(
        jnp.bfloat16
    )
    up_grad = (hidden_grad * activated).astype(jnp.bfloat16)
    down_total = lax.dot_general(
        hidden, pair_scaled, contract_rows, preferred_element_type=jnp.float32
    )
    gate_total = lax.dot_general(
        pair_inputs, gate_grad, contract_rows, preferred_element_type=jnp.float32
    )
    up_total = lax.dot_general(
        pair_inputs, up_grad, contract_rows, preferred_element_type=jnp.float32
    )
    partial_back = lax.dot_general(
        gate_grad, gate_slice, contract_last, preferred_element_type=jnp.float32
    )
    partial_back = partial_back + lax.dot_general(
        up_grad, up_slice, contract_last, preferred_element_type=jnp.float32
    )
    return (partial_back, gate_total, up_total, down_total)


def per_device(incoming, stash, expert_ids, route_weight, w_gate, w_up, w_down):
    arrived = passed_along(incoming, "section", -1)
    upstream = arrived[0]
    tokens = stash[0]
    mbatch, tok_rows, model_width = tokens.shape
    top_count = expert_ids.shape[-1]
    experts = lax.axis_size("expert")
    replicas = lax.axis_size("dp")
    groups = replicas * experts
    capacity = max(2, 3 * tok_rows * top_count // (2 * experts))
    pair_count = tok_rows * top_count
    chosen = expert_ids[0].reshape(mbatch, pair_count)
    onehot = (chosen[:, :, None] == jnp.arange(experts, dtype=jnp.int32)[None, None, :]).astype(
        jnp.int32
    )
    running = jnp.cumsum(onehot, axis=1) - 1
    position = jnp.sum(onehot * running, axis=2)
    slot_index = chosen * capacity + position
    batch_index = jnp.arange(mbatch, dtype=jnp.int32)[:, None]
    pair_inputs = jnp.repeat(tokens, top_count, axis=1)
    weight_pairs = route_weight[0].reshape(mbatch, pair_count)
    pair_scaled = (
        weight_pairs[:, :, None] * jnp.repeat(upstream, top_count, axis=1).astype(jnp.float32)
    ).astype(jnp.bfloat16)
    empty_slots = jnp.zeros((mbatch, experts * capacity, model_width), jnp.bfloat16)
    input_slots = (
        empty_slots.at[batch_index, slot_index]
        .set(pair_inputs)
        .reshape(mbatch, experts, capacity, model_width)
    )
    scaled_slots = (
        empty_slots.at[batch_index, slot_index]
        .set(pair_scaled)
        .reshape(mbatch, experts, capacity, model_width)
    )
    tiled_shape = (mbatch, replicas, experts, capacity, model_width)
    tiled_inputs = jnp.broadcast_to(input_slots[:, None], tiled_shape).reshape(
        mbatch, groups, capacity, model_width
    )
    tiled_scaled = jnp.broadcast_to(scaled_slots[:, None], tiled_shape).reshape(
        mbatch, groups, capacity, model_width
    )
    recv_inputs, recv_scaled = (
        lax.all_to_all(tiled_inputs, ("dp", "expert"), split_axis=1, concat_axis=1, tiled=True),
        lax.all_to_all(tiled_scaled, ("dp", "expert"), split_axis=1, concat_axis=1, tiled=True),
    )
    row_total = mbatch * groups * capacity
    input_rows = recv_inputs.reshape(row_total, model_width)
    scaled_rows = recv_scaled.reshape(row_total, model_width)
    gate_slice = w_gate[0, 0]
    up_slice = w_up[0, 0]
    down_slice = w_down[0, 0]
    partial_rows, gate_total, up_total, down_total = slice_backward(
        input_rows, scaled_rows, gate_slice, up_slice, down_slice
    )
    sent_back = partial_rows.astype(jnp.bfloat16).reshape(mbatch, groups, capacity, model_width)
    returned = lax.all_to_all(sent_back, ("dp", "expert"), split_axis=1, concat_axis=1, tiled=True)
    summed = jnp.sum(
        returned.reshape(mbatch, replicas, experts, capacity, model_width).astype(jnp.float32),
        axis=1,
    )
    pair_back = lax.optimization_barrier(summed.astype(jnp.bfloat16))
    back_flat = pair_back.reshape(mbatch, experts * capacity, model_width)
    per_pair = (
        back_flat[batch_index, slot_index]
        .astype(jnp.float32)
        .reshape(mbatch, tok_rows, top_count, model_width)
    )
    input_grad = (upstream.astype(jnp.float32) + jnp.sum(per_pair, axis=2)).astype(jnp.bfloat16)
    grad_gate = gate_total.astype(jnp.bfloat16)[None, None]
    grad_up = up_total.astype(jnp.bfloat16)[None, None]
    grad_down = down_total.astype(jnp.bfloat16)[None, None]
    return (input_grad[None], grad_gate, grad_up, grad_down)


def solution(mesh):
    return jax.shard_map(
        per_device,
        mesh=mesh,
        in_specs=(
            P("section", None, ("dp", "expert"), None),
            P("section", None, ("dp", "expert"), None),
            P("section", None, ("dp", "expert"), None),
            P("section", None, ("dp", "expert"), None),
            P("section", "expert", None, "dp"),
            P("section", "expert", None, "dp"),
            P("section", "expert", "dp", None),
        ),
        out_specs=(
            P("section", None, ("dp", "expert"), None),
            P("section", "expert", None, "dp"),
            P("section", "expert", None, "dp"),
            P("section", "expert", "dp", None),
        ),
        check_vma=False,
    )
```

profile of v0, /device:TPU:0, one launch (start us, length us, event | category | flops | bytes accessed | tf_op | source)
XLA Modules:
  0.0 163.9 jit_solution(9056116287061586994)
XLA Ops:
  1.3 0.8 copy.29
  2.8 1.2 broadcast_in_dim.54
  4.2 9.1 %scatter_fusion.1 = bf16[2,48,3584]{2,1,0:T(8,128)(2,1)S(1)} fusion(bf16[2,48,3584]{2,1,0:T(8,128)(2,1)S(1)} %broadcast_in_dim.22.clone, s32[64]{0:T(128)S(1)} %reshape.91, bf16[64,3584]{1,0:T(8,128)(2,1)S(1)} %reshape.99), kind=kCustom, calls=%fused_computation.2 | custom fusion | bytes 1376768 | tf_op jit(solution)/shard_map/scatter | solution.py:72
  13.3 0.7 copy.33
  14.1 1.8 %broadcast_in_dim.56 = bf16[2,2,4,12,3584]{4,0,3,2,1:T(2,128)(2,1)} broadcast(bf16[2,4,12,3584]{3,0,2,1:T(2,128)(2,1)S(1)} %bitcast.73), dimensions={0,2,3,4} | broadcast | bytes 2064384 | tf_op jit(solution)/shard_map/broadcast_in_dim | solution.py:81
  15.9 7.3 %all-to-all-start.1 = ((bf16[2,8,12,3584]{3,0,2,1:T(2,128)(2,1)}), bf16[2,8,12,3584]{3,0,2,1:T(2,128)(2,1)S(1)}, u32[]{:S(2)}, u32[]{:S(2)}) async-start(bf16[2,8,12,3584]{3,0,2,1:T(2,128)(2,1)} %bitcast.8), calls=%async_computation.1 | async-start | bytes 2752512 | tf_op jit(solution)/shard_map/all_to_all | solution.py:88
  23.2 0.7 collective-permute-start
  24.1 3.4 %collective-permute-done = bf16[1,2,16,3584]{3,2,1,0:T(8,128)(2,1)S(1)} collective-permute-done((bf16[1,2,16,3584]{3,2,1,0:T(8,128)(2,1)S(1)}, bf16[1,2,16,3584]{3,2,1,0:T(8,128)(2,1)S(1)}, u32[]{:S(2)}, u32[]{:S(2)}) %collective-permute-start) | collective-permute-done | bytes 229408 | tf_op jit(solution)/shard_map/ppermute | solution.py:9
  29.2 9.1 %scatter_fusion = bf16[2,48,3584]{2,1,0:T(8,128)(2,1)S(1)} fusion(bf16[2,48,3584]{2,1,0:T(8,128)(2,1)S(1)} %broadcast_in_dim.22.clone.1, s32[64]{0:T(128)S(1)} %reshape.91, bf16[64,3584]{1,0:T(8,128)(2,1)S(1)} %bitcast.75), kind=kCustom, calls=%fused_computation.1 | custom fusion | bytes 1376768 | tf_op jit(solution)/shard_map/scatter | solution.py:77
  38.4 0.7 copy.31
  39.1 17.7 %all-to-all-done.1 = bf16[2,8,12,3584]{3,0,2,1:T(2,128)(2,1)S(1)} async-done(((bf16[2,8,12,3584]{3,0,2,1:T(2,128)(2,1)}), bf16[2,8,12,3584]{3,0,2,1:T(2,128)(2,1)S(1)}, u32[]{:S(2)}, u32[]{:S(2)}) %all-to-all-start.1) | async-done | bytes 1376288 | tf_op jit(solution)/shard_map/all_to_all | solution.py:88
  56.8 1.8 %broadcast_in_dim.26 = bf16[2,2,4,12,3584]{4,0,3,2,1:T(2,128)(2,1)} broadcast(bf16[2,4,12,3584]{3,0,2,1:T(2,128)(2,1)S(1)} %bitcast.72), dimensions={0,2,3,4} | broadcast | bytes 2064384 | tf_op jit(solution)/shard_map/broadcast_in_dim | solution.py:84
  58.6 4.4 %all-to-all-start = ((bf16[2,8,12,3584]{3,0,2,1:T(2,128)(2,1)}), bf16[2,8,12,3584]{3,0,2,1:T(2,128)(2,1)}, u32[]{:S(2)}, u32[]{:S(2)}) async-start(bf16[2,8,12,3584]{3,0,2,1:T(2,128)(2,1)} %bitcast.4), calls=%async_computation | async-start | bytes 2752512 | tf_op jit(solution)/shard_map/all_to_all | solution.py:89
  63.7 6.1 %fusion.2 = f32[192,1024]{1,0:T(8,128)} fusion(bf16[192,3584]{1,0:T(8,128)(2,1)S(1)} %reshape.79, bf16[1,1,3584,1024]{3,2,1,0:T(8,128)(2,1)} %param.11), kind=kOutput, calls=%fused_computation.8 | convolution fusion | flops 1409286144 | bytes 9502720 | tf_op jit(solution)/shard_map/dot_general | solution.py:15
  69.7 5.6 %fusion.6 = f32[192,1024]{1,0:T(8,128)} fusion(bf16[192,3584]{1,0:T(8,128)(2,1)S(1)} %reshape.79, bf16[1,1,3584,1024]{3,2,1,0:T(8,128)(2,1)} %param.12), kind=kOutput, calls=%fused_computation.12 | convolution fusion | flops 1409286144 | bytes 9502720 | tf_op jit(solution)/shard_map/dot_general | solution.py:16
  75.3 20.3 %all-to-all-done = bf16[2,8,12,3584]{3,0,2,1:T(2,128)(2,1)} async-done(((bf16[2,8,12,3584]{3,0,2,1:T(2,128)(2,1)}), bf16[2,8,12,3584]{3,0,2,1:T(2,128)(2,1)}, u32[]{:S(2)}, u32[]{:S(2)}) %all-to-all-start) | async-done | bytes 1376288 | tf_op jit(solution)/shard_map/all_to_all | solution.py:89
  95.6 2.8 %copy.32 = bf16[2,8,12,3584]{3,2,1,0:T(8,128)(2,1)} copy(bf16[2,8,12,3584]{3,0,2,1:T(2,128)(2,1)} %all-to-all-done) | data formatting | bytes 2752512 | tf_op jit(solution)/shard_map/all_to_all | solution.py:89
  98.4 3.6 %reshape.76 = bf16[192,3584]{1,0:T(8,128)(2,1)} reshape(bf16[2,8,12,3584]{3,2,1,0:T(8,128)(2,1)} %copy.32) | data formatting | bytes 2752512 | tf_op jit(solution)/shard_map/reshape | solution.py:93
  102.0 6.5 %multiply_convert_fusion.2 = (bf16[192,1024]{1,0:T(8,128)(2,1)S(1)}, bf16[192,1024]{1,0:T(8,128)(2,1)S(1)}) fusion(f32[192,1024]{1,0:T(8,128)} %fusion.2, f32[192,1024]{1,0:T(8,128)} %fusion.6, bf16[192,3584]{1,0:T(8,128)(2,1)} %reshape.76, bf16[1,1,1024,3584]{3,2,1,0:T(8,128)(2,1)} %param.13), kind=kOutput, calls=%fused_computation.23 | convolution fusion | flops 1411842048 | bytes 11075584 | tf_op jit(solution)/shard_map/dot_general | solution.py:20
  108.6 2.6 %fusion = f32[192,3584]{1,0:T(8,128)S(1)} fusion(bf16[192,1024]{1,0:T(8,128)(2,1)S(1)} %get-tuple-element.5, bf16[1,1,3584,1024]{3,2,1,0:T(8,128)(2,1)S(1)} %bitcast.70), kind=kOutput, calls=%fused_computation.6 | convolution fusion | flops 1409286144 | bytes 10485760 | tf_op jit(solution)/shard_map/dot_general | solution.py:36
  111.2 5.6 %fusion.16 = bf16[192,3584]{1,0:T(8,128)(2,1)S(1)} fusion(f32[192,3584]{1,0:T(8,128)S(1)} %fusion, bf16[192,1024]{1,0:T(8,128)(2,1)S(1)} %get-tuple-element.4, bf16[1,1,3584,1024]{3,2,1,0:T(8,128)(2,1)} %param.12), kind=kOutput, calls=%fused_computation.20 | convolution fusion | flops 1410662400 | bytes 11862016 | tf_op jit(solution)/shard_map/dot_general | solution.py:39
  117.2 2.5 %copy.35 = bf16[2,8,12,3584]{3,0,2,1:T(2,128)(2,1)} copy(bf16[2,8,12,3584]{3,2,1,0:T(8,128)(2,1)S(1)} %reshape.80) | data formatting | bytes 2752512 | tf_op jit(solution)/shard_map/reshape | solution.py:100
  119.7 3.8 %all-to-all-start.2 = ((bf16[2,8,12,3584]{3,0,2,1:T(2,128)(2,1)}), bf16[2,8,12,3584]{3,0,2,1:T(2,128)(2,1)S(1)}, u32[]{:S(2)}, u32[]{:S(2)}) async-start(bf16[2,8,12,3584]{3,0,2,1:T(2,128)(2,1)} %copy.35), calls=%async_computation.2 | async-start | bytes 2752512 | tf_op jit(solution)/shard_map/all_to_all | solution.py:101
  123.6 6.2 %fusion.11 = bf16[1,1,3584,1024]{3,2,1,0:T(8,128)(2,1)} fusion(bf16[192,3584]{1,0:T(8,128)(2,1)S(1)} %copy-done.2, bf16[192,1024]{1,0:T(8,128)(2,1)} %copy-done.9), kind=kOutput, calls=%fused_computation.17 | convolution fusion | flops 1412956160 | bytes 9109504 | tf_op jit(solution)/shard_map/dot_general | solution.py:33
  129.9 5.2 %fusion.10 = bf16[1,1,3584,1024]{3,2,1,0:T(8,128)(2,1)} fusion(bf16[192,3584]{1,0:T(8,128)(2,1)S(1)} %copy-done.2, bf16[192,1024]{1,0:T(8,128)(2,1)S(1)} %copy-done.8), kind=kOutput, calls=%fused_computation.16 | convolution fusion | flops 1412956160 | bytes 9109504 | tf_op jit(solution)/shard_map/dot_general | solution.py:30
  135.1 5.2 %fusion.12 = bf16[1,1,1024,3584]{3,2,1,0:T(8,128)(2,1)} fusion(bf16[192,3584]{1,0:T(8,128)(2,1)S(1)} %copy-done, f32[192,1024]{1,0:T(8,128)S(1)} %copy-done.4, f32[192,1024]{1,0:T(8,128)S(1)} %copy-done.3), kind=kOutput, calls=%fused_computation.18 | convolution fusion | flops 1414135808 | bytes 10289152 | tf_op jit(solution)/shard_map/dot_general | solution.py:27
  140.3 15.2 %all-to-all-done.2 = bf16[2,8,12,3584]{3,0,2,1:T(2,128)(2,1)S(1)} async-done(((bf16[2,8,12,3584]{3,0,2,1:T(2,128)(2,1)}), bf16[2,8,12,3584]{3,0,2,1:T(2,128)(2,1)S(1)}, u32[]{:S(2)}, u32[]{:S(2)}) %all-to-all-start.2) | async-done | bytes 1376288 | tf_op jit(solution)/shard_map/all_to_all | solution.py:101
  155.5 3.1 %reduce_sum.36 = bf16[2,4,12,3584]{3,0,2,1:T(2,128)(2,1)S(1)} reduce(bf16[2,2,4,12,3584]{4,0,3,2,1:T(2,128)(2,1)S(1)} %bitcast.71, bf16[]{:T(256)} %constant.7.clone.1), dimensions={1}, to_apply=%region_4.5 | reduce | flops 344064 | bytes 2064386 | tf_op jit(solution)/shard_map/reduce_sum | solution.py:102
  158.7 0.7 copy.37
  159.5 2.0 %gather_fusion = bf16[64,3584]{1,0:T(8,128)(2,1)S(1)} fusion(bf16[2,48,3584]{2,1,0:T(8,128)(2,1)S(1)} %copy.38, s32[64]{0:T(128)S(1)} %reshape.85), kind=kCustom, calls=%fused_computation | custom fusion | bytes 918016 | tf_op jit(solution)/shard_map/gather | solution.py:109
  162.1 1.1 reduce_sum.37
  163.2 0.7 fusion.20
  (54 shorter events, 5.4 us)
Async XLA Ops:
  14.1 9.1 %copy-start.11 = (bf16[1,2,16,3584]{3,2,1,0:T(8,128)(2,1)S(1)}, bf16[1,2,16,3584]{3,2,1,0:T(8,128)(2,1)}, u32[]{:S(2)}) copy-start(bf16[1,2,16,3584]{3,2,1,0:T(8,128)(2,1)} %param.7) | copy-start | bytes 688132
  14.1 9.8 %copy-start.10 = (f32[1,2,16,2]{2,3,1,0:T(2,128)S(1)}, f32[1,2,16,2]{2,3,1,0:T(2,128)}, u32[]{:S(2)}) copy-start(f32[1,2,16,2]{2,3,1,0:T(2,128)} %param.10) | copy-start | bytes 772
  15.9 40.9 %all-to-all-start.1 = ((bf16[2,8,12,3584]{3,0,2,1:T(2,128)(2,1)}), bf16[2,8,12,3584]{3,0,2,1:T(2,128)(2,1)S(1)}, u32[]{:S(2)}, u32[]{:S(2)}) async-start(bf16[2,8,12,3584]{3,0,2,1:T(2,128)(2,1)} %bitcast.8), calls=%async_computation.1 | async-start | bytes 2752512 | tf_op jit(solution)/shard_map/all_to_all | solution.py:88
  23.2 4.2 %collective-permute-start = (bf16[1,2,16,3584]{3,2,1,0:T(8,128)(2,1)S(1)}, bf16[1,2,16,3584]{3,2,1,0:T(8,128)(2,1)S(1)}, u32[]{:S(2)}, u32[]{:S(2)}) collective-permute-start(bf16[1,2,16,3584]{3,2,1,0:T(8,128)(2,1)S(1)} %copy-done.11), channel_id=1, source_target_pairs={{0,24},{8,0},{16,8},{24,16},{1,25},{9,1},{17,9},{25,17},{2,26},{10... | collective-permute-start | bytes 688136 | tf_op jit(solution)/shard_map/ppermute | solution.py:9
  27.4 0.7 copy-start.5
  58.6 37.0 %all-to-all-start = ((bf16[2,8,12,3584]{3,0,2,1:T(2,128)(2,1)}), bf16[2,8,12,3584]{3,0,2,1:T(2,128)(2,1)}, u32[]{:S(2)}, u32[]{:S(2)}) async-start(bf16[2,8,12,3584]{3,0,2,1:T(2,128)(2,1)} %bitcast.4), calls=%async_computation | async-start | bytes 2752512 | tf_op jit(solution)/shard_map/all_to_all | solution.py:89
  63.7 6.1 %copy-start.1 = (bf16[192,3584]{1,0:T(8,128)(2,1)}, bf16[192,3584]{1,0:T(8,128)(2,1)S(1)}, u32[]{:S(2)}) copy-start(bf16[192,3584]{1,0:T(8,128)(2,1)S(1)} %reshape.79) | copy-start | bytes 4128772
  98.4 10.1 %slice-start = ((s8[7340032]{0:T(1024)(128)(4,1)}), s8[3145728]{0:T(1024)(128)(4,1)S(1)}, s32[]{:S(2)}) async-start(s8[7340032]{0:T(1024)(128)(4,1)} %bitcast.69), calls=%async_computation.3 | async-start | bytes 6291456
  102.0 6.6 %slice-start.1 = ((s8[7340032]{0:T(1024)(128)(4,1)}), s8[4194304]{0:T(1024)(128)(4,1)S(1)}, s32[]{:S(2)}) async-start(s8[7340032]{0:T(1024)(128)(4,1)} %bitcast.69), calls=%async_computation.4 | async-start | bytes 8388608
  108.5 2.6 %copy-start.7 = (bf16[192,1024]{1,0:T(8,128)(2,1)}, bf16[192,1024]{1,0:T(8,128)(2,1)S(1)}, u32[]{:S(2)}) copy-start(bf16[192,1024]{1,0:T(8,128)(2,1)S(1)} %get-tuple-element.5) | copy-start | bytes 1179652
  108.6 2.6 %copy-start.9 = (bf16[192,1024]{1,0:T(8,128)(2,1)}, bf16[192,1024]{1,0:T(8,128)(2,1)S(1)}, u32[]{:S(2)}) copy-start(bf16[192,1024]{1,0:T(8,128)(2,1)S(1)} %get-tuple-element.4) | copy-start | bytes 1179652
  117.2 6.4 %copy-start.2 = (bf16[192,3584]{1,0:T(8,128)(2,1)S(1)}, bf16[192,3584]{1,0:T(8,128)(2,1)}, u32[]{:S(2)}) copy-start(bf16[192,3584]{1,0:T(8,128)(2,1)} %copy-done.1) | copy-start | bytes 4128772
  119.7 35.7 %all-to-all-start.2 = ((bf16[2,8,12,3584]{3,0,2,1:T(2,128)(2,1)}), bf16[2,8,12,3584]{3,0,2,1:T(2,128)(2,1)S(1)}, u32[]{:S(2)}, u32[]{:S(2)}) async-start(bf16[2,8,12,3584]{3,0,2,1:T(2,128)(2,1)} %copy.35), calls=%async_computation.2 | async-start | bytes 2752512 | tf_op jit(solution)/shard_map/all_to_all | solution.py:101
  123.6 6.2 %copy-start.8 = (bf16[192,1024]{1,0:T(8,128)(2,1)S(1)}, bf16[192,1024]{1,0:T(8,128)(2,1)}, u32[]{:S(2)}) copy-start(bf16[192,1024]{1,0:T(8,128)(2,1)} %copy-done.7) | copy-start | bytes 1179652
  129.9 5.2 %copy-start = (bf16[192,3584]{1,0:T(8,128)(2,1)S(1)}, bf16[192,3584]{1,0:T(8,128)(2,1)}, u32[]{:S(2)}) copy-start(bf16[192,3584]{1,0:T(8,128)(2,1)} %reshape.76) | copy-start | bytes 4128772
  129.9 5.2 %copy-start.3 = (f32[192,1024]{1,0:T(8,128)S(1)}, f32[192,1024]{1,0:T(8,128)}, u32[]{:S(2)}) copy-start(f32[192,1024]{1,0:T(8,128)} %fusion.2) | copy-start | bytes 2359300
  129.9 5.2 %copy-start.4 = (f32[192,1024]{1,0:T(8,128)S(1)}, f32[192,1024]{1,0:T(8,128)}, u32[]{:S(2)}) copy-start(f32[192,1024]{1,0:T(8,128)} %fusion.6) | copy-start | bytes 2359300
  159.4 3.7 %copy-start.6 = (bf16[1,2,16,3584]{3,2,1,0:T(8,128)(2,1)S(1)}, bf16[1,2,16,3584]{3,2,1,0:T(8,128)(2,1)}, u32[]{:S(2)}) copy-start(bf16[1,2,16,3584]{3,2,1,0:T(8,128)(2,1)} %copy-done.5) | copy-start | bytes 688132
where the time goes:
time: 164 us
  waiting for transfers between devices  56.6 us (35%)
  matrix products  43 us (26%)
  local copies, waits for them, and re-layouts  41.1 us (25%)
  starting transfers between devices  16.2 us (10%)
  other arithmetic  6.04 us (4%)
    all_to_all x1, waiting for transfers between devices, per_device(): lax.all_to_all(tiled_scaled, ('dp', 'expert'), split_axis=1, concat_axis=...  20.3 us
    all_to_all x1, waiting for transfers between devices, per_device(): lax.all_to_all(tiled_inputs, ('dp', 'expert'), split_axis=1, concat_axis=...  17.7 us
    all_to_all x1, waiting for transfers between devices, per_device(): lax.all_to_all(sent_back, ('dp', 'expert'), split_axis=1, concat_axis=1,...  15.2 us
    scatter x2, local copies, waits for them, and re-layouts, per_device(): input_slots = empty_slots.at[batch_index, slot_index].set(pair_inputs).re...  9.86 us
    scatter x2, local copies, waits for them, and re-layouts, per_device(): scaled_slots = empty_slots.at[batch_index, slot_index].set(pair_scaled).r...  9.86 us
    all_to_all x1, starting transfers between devices, per_device(): lax.all_to_all(tiled_inputs, ('dp', 'expert'), split_axis=1, concat_axis=...  7.28 us
    dot_general x1, matrix products, slice_backward(): lax.dot_general(pair_scaled, down_slice, contract_last, preferred_element...  6.53 us
    dot_general x1, matrix products, slice_backward(): lax.dot_general(pair_inputs, up_grad, contract_rows, preferred_element_ty...  6.23 us
  transfers between devices with their start and end apart: 4, of which 4 were waited for; matrix products, arithmetic and copies ran while one was open for 24% of the time, Pallas kernels for 0%

commit v1 on v0

v1 whole, which is shorter than its diff:
```python
import jax
import jax.numpy as jnp
from jax import lax
from jax.sharding import PartitionSpec as P


def passed_along(x, axis, by):
    length = lax.axis_size(axis)
    return lax.ppermute(x, axis, [(i, (i + by) % length) for i in range(length)])


def per_device(incoming, stash, expert_ids, route_weight, w_gate, w_up, w_down):
    group = ("dp", "expert")
    mbatch, tok_rows, width = stash.shape[1:]
    rows = mbatch * tok_rows
    mine = lax.axis_index("expert")
    own_tokens = stash[0].reshape(rows, width)
    upstream = passed_along(incoming[0].reshape(rows, width), "section", -1)
    experts = lax.axis_size("expert")
    named = expert_ids[0][..., None] == jnp.arange(experts, dtype=jnp.int32)
    token_weight = jnp.sum(
        jnp.where(named, route_weight[0][..., None], 0.0), axis=2
    ).reshape(rows, experts)
    all_weight = lax.all_gather(token_weight, group, axis=0, tiled=True)
    tokens = lax.all_gather(own_tokens, group, axis=0, tiled=True)
    ups = lax.all_gather(upstream, group, axis=0, tiled=True)
    weight = lax.dynamic_slice_in_dim(all_weight, mine, 1, axis=1)
    gate_slice, up_slice, down_slice = w_gate[0, 0], w_up[0, 0], w_down[0, 0]
    contract_rows = (((0,), (0,)), ((), ()))
    contract_last = (((1,), (1,)), ((), ()))
    f32 = jnp.float32
    gate_pre = jnp.dot(tokens, gate_slice, preferred_element_type=f32)
    up_pre = jnp.dot(tokens, up_slice, preferred_element_type=f32)
    logistic = jax.nn.sigmoid(gate_pre)
    activated = gate_pre * logistic
    hidden = (activated * up_pre).astype(jnp.bfloat16)
    scaled = (weight * ups.astype(f32)).astype(jnp.bfloat16)
    hidden_grad = lax.dot_general(scaled, down_slice, contract_last, preferred_element_type=f32)
    gate_grad = (hidden_grad * up_pre * logistic * (1.0 + gate_pre * (1.0 - logistic))).astype(
        jnp.bfloat16
    )
    up_grad = (hidden_grad * activated).astype(jnp.bfloat16)
    back = lax.dot_general(gate_grad, gate_slice, contract_last, preferred_element_type=f32)
    back = back + lax.dot_general(up_grad, up_slice, contract_last, preferred_element_type=f32)
    summed = lax.psum_scatter(
        back.astype(jnp.bfloat16), group, scatter_dimension=0, tiled=True
    )
    grad_down = lax.dot_general(hidden, scaled, contract_rows, preferred_element_type=f32)
    grad_gate = lax.dot_general(tokens, gate_grad, contract_rows, preferred_element_type=f32)
    grad_up = lax.dot_general(tokens, up_grad, contract_rows, preferred_element_type=f32)
    input_grad = (upstream.astype(f32) + summed.astype(f32)).astype(jnp.bfloat16)
    return (
        input_grad.reshape(1, mbatch, tok_rows, width),
        grad_gate.astype(jnp.bfloat16)[None, None],
        grad_up.astype(jnp.bfloat16)[None, None],
        grad_down.astype(jnp.bfloat16)[None, None],
    )


def solution(mesh):
    tokens = P("section", None, ("dp", "expert"), None)
    columns = P("section", "expert", None, "dp")
    rows = P("section", "expert", "dp", None)
    return jax.shard_map(
        per_device,
        mesh=mesh,
        in_specs=(tokens, tokens, tokens, tokens, columns, columns, rows),
        out_specs=(tokens, columns, columns, rows),
        check_vma=False,
    )
```

time: 164 us -> 197 us (1.20)
  blocking collectives: 0 us -> 27.3 us
  waiting for transfers between devices: 56.6 us -> 82.8 us
  local copies, waits for them, and re-layouts: 41.1 us -> 21.9 us
  starting transfers between devices: 16.2 us -> 2.55 us
  between operations: 0.95 us -> 13.8 us
  other arithmetic: 6.04 us -> 2.39 us
  matrix products: 43 us -> 45.5 us
    all_to_all x3 -> x0, waiting for transfers between devices: 53.2 us -> none  [the longest x1 20.3 us: per_device(): lax.all_to_all(tiled_scaled, ('dp', 'expert'), split_axis=1, concat_axis=...]
    all_gather x0 -> x2, waiting for transfers between devices: none -> 50.9 us  [the longest x1 35.1 us: per_device(): ups = lax.all_gather(upstream, group, axis=0, tiled=True)]
    all_gather x0 -> x1, blocking collectives: none -> 27.3 us  [per_device(): all_weight = lax.all_gather(token_weight, group, axis=0, tiled=True)]
    reduce_scatter x0 -> x1, waiting for transfers between devices: none -> 27.3 us  [per_device(): lax.psum_scatter(back.astype(jnp.bfloat16), group, scatter_dimension=0, t...]
    unnamed x31 -> x14, local copies, waits for them, and re-layouts: 1.66 us -> 21.8 us
    scatter x4 -> x0, local copies, waits for them, and re-layouts: 19.7 us -> none  [the longest x2 9.86 us: per_device(): input_slots = empty_slots.at[batch_index, slot_index].set(pair_inputs).re...]
    all_to_all x3 -> x0, starting transfers between devices: 15.5 us -> none  [the longest x1 7.28 us: per_device(): lax.all_to_all(tiled_inputs, ('dp', 'expert'), split_axis=1, concat_axis=...]
    reshape x6 -> x0, local copies, waits for them, and re-layouts: 7.05 us -> none  [the longest x1 3.57 us: per_device(): scaled_rows = recv_scaled.reshape(row_total, model_width)]
  transfers between devices with their start and end apart: 4 -> 4, of which waited for: 4 -> 4; matrix products, arithmetic and copies ran while one was open for 24% -> 27% of each run, Pallas kernels for 0% -> 0%
where the time goes in v1:
time: 197 us; the launch traced here: 196 us
  waiting for transfers between devices  82.8 us (42%)
  matrix products  45.5 us (23%)
  blocking collectives  27.3 us (14%)
  local copies, waits for them, and re-layouts  21.9 us (11%)
  between operations  13.8 us (7%)
  starting transfers between devices  2.55 us (1%)
  other arithmetic  2.39 us (1%)
    all_gather x1, waiting for transfers between devices, per_device(): ups = lax.all_gather(upstream, group, axis=0, tiled=True)  35.1 us
    all_gather x1, blocking collectives, per_device(): all_weight = lax.all_gather(token_weight, group, axis=0, tiled=True)  27.3 us
    reduce_scatter x1, waiting for transfers between devices, per_device(): lax.psum_scatter(back.astype(jnp.bfloat16), group, scatter_dimension=0, t...  27.3 us
    unnamed x14, local copies, waits for them, and re-layouts  21.8 us
    all_gather x1, waiting for transfers between devices, per_device(): tokens = lax.all_gather(own_tokens, group, axis=0, tiled=True)  15.9 us
    dot_general x1, matrix products, per_device(): lax.dot_general(hidden, scaled, contract_rows, preferred_element_type=f32)  6.95 us
    dot_general x1, matrix products, per_device(): gate_pre = jnp.dot(tokens, gate_slice, preferred_element_type=f32)  6.82 us
    dot_general x1, matrix products, per_device(): lax.dot_general(scaled, down_slice, contract_last, preferred_element_type...  6.59 us
  transfers between devices with their start and end apart: 4, of which 4 were waited for; matrix products, arithmetic and copies ran while one was open for 27% of the time, Pallas kernels for 0%

profile of v1, /device:TPU:0, one launch (start us, length us, event | category | flops | bytes accessed | tf_op | source)
XLA Modules:
  0.0 196.2 jit_solution(9397855366287876503)
XLA Ops:
  7.2 0.0 all-gather.6.cloned.1.call-start
  7.2 0.7 all-gather.6.cloned.1.call-update
  7.9 0.0 all-gather.4.cloned.1.call-start
  7.9 2.4 %collective-permute-start = (bf16[32,3584]{1,0:T(8,128)(2,1)}, bf16[32,3584]{1,0:T(8,128)(2,1)S(1)}, u32[]{:S(2)}, u32[]{:S(2)}) collective-permute-start(bf16[32,3584]{1,0:T(8,128)(2,1)} %bitcast.53), channel_id=1, source_target_pairs={{0,24},{8,0},{16,8},{24,16},{1,25},{9,1},{17,9},{25,17},{2,26},{10... | collective-permute-start | bytes 688136 | tf_op jit(solution)/shard_map/ppermute | solution.py:9
  10.4 3.9 %collective-permute-done = bf16[32,3584]{1,0:T(8,128)(2,1)S(1)} collective-permute-done((bf16[32,3584]{1,0:T(8,128)(2,1)}, bf16[32,3584]{1,0:T(8,128)(2,1)S(1)}, u32[]{:S(2)}, u32[]{:S(2)}) %collective-permute-start) | collective-permute-done | bytes 229408 | tf_op jit(solution)/shard_map/ppermute | solution.py:9
  14.2 0.0 copy-start.1
  14.2 0.7 copy-done.1
  14.9 0.0 all-gather.4.cloned.1.call-update
  14.9 0.0 reduce-scatter.2.cloned.1.call-start
  15.0 0.7 select_reduce_fusion
  15.7 0.1 reshape.18
  15.8 27.3 %all-gather = f32[8,32,4]{1,2,0:T(4,128)S(1)} all-gather(f32[1,32,4]{1,2,0:T(4,128)S(1)} %reshape.18), channel_id=1, replica_groups=mesh['section'=4,'dp'=2,'expert'=4] {'dp','expert'}, dimensions={0}, use_global_device_ids=true | all-gather | bytes 4608 | tf_op jit(solution)/shard_map/all_gather | solution.py:24
  43.1 0.1 reshape.19
  43.2 15.9 %all-gather.6.cloned.1.call-done = bf16[256,3584]{1,0:T(8,128)(2,1)} async-done(((bf16[32,3584]{1,0:T(8,128)(2,1)}), bf16[256,3584]{1,0:T(8,128)(2,1)}) %all-gather.6.cloned.1.call-update) | async-done | bytes 1835024 | tf_op jit(solution)/shard_map/all_gather | solution.py:25
  59.1 6.8 %fusion.2 = f32[256,1024]{1,0:T(8,128)} fusion(bf16[256,3584]{1,0:T(8,128)(2,1)} %all-gather.6.cloned.1.call-done, bf16[1,1,3584,1024]{3,2,1,0:T(8,128)(2,1)} %param.11), kind=kOutput, calls=%fused_computation.5 | convolution fusion | flops 1879048192 | bytes 10223616 | tf_op jit(solution)/shard_map/dot_general | solution.py:32
  65.9 0.0 copy-done
  65.9 6.3 %fusion.6 = f32[256,1024]{1,0:T(8,128)} fusion(bf16[256,3584]{1,0:T(8,128)(2,1)S(1)} %copy-done, bf16[1,1,3584,1024]{3,2,1,0:T(8,128)(2,1)} %param.12), kind=kOutput, calls=%fused_computation.9 | convolution fusion | flops 1879048192 | bytes 10223616 | tf_op jit(solution)/shard_map/dot_general | solution.py:33
  72.2 35.1 %all-gather.4.cloned.1.call-done = bf16[256,3584]{1,0:T(8,128)(2,1)} async-done(((bf16[32,3584]{1,0:T(8,128)(2,1)}), bf16[256,3584]{1,0:T(8,128)(2,1)}) %all-gather.4.cloned.1.call-update) | async-done | bytes 1835024 | tf_op jit(solution)/shard_map/all_gather | solution.py:26
  107.3 6.6 %multiply_convert_fusion.2 = (bf16[256,1024]{1,0:T(8,128)(2,1)S(1)}, bf16[256,1024]{1,0:T(8,128)(2,1)S(1)}) fusion(f32[256,1024]{1,0:T(8,128)} %fusion.2, f32[256,1024]{1,0:T(8,128)} %fusion.6, bf16[1,1,1024,3584]{3,2,1,0:T(8,128)(2,1)} %param.13, bf16[256,3584]{1,0:T(8,128)(2,1)} %all-gather.4.cloned.1.call-done, f32[256]{0:T(256)S(1)} %bitcast.51), kind=kOutput, calls=%fused_computation.20 | convolution fusion | flops 1885208576 | bytes 12321792 | tf_op jit(solution)/shard_map/dot_general | solution.py:38
  113.9 0.0 copy-done.3
  113.9 2.1 %fusion = f32[256,3584]{1,0:T(8,128)S(1)} fusion(bf16[256,1024]{1,0:T(8,128)(2,1)S(1)} %get-tuple-element.21, bf16[1,1,3584,1024]{3,2,1,0:T(8,128)(2,1)S(1)} %copy-done.3), kind=kOutput, calls=%fused_computation.3 | convolution fusion | flops 1879048192 | bytes 11534336 | tf_op jit(solution)/shard_map/dot_general | solution.py:43
  116.0 6.4 %fusion.16 = bf16[256,3584]{1,0:T(8,128)(2,1)} fusion(f32[256,3584]{1,0:T(8,128)S(1)} %fusion, bf16[256,1024]{1,0:T(8,128)(2,1)S(1)} %get-tuple-element.20, bf16[1,1,3584,1024]{3,2,1,0:T(8,128)(2,1)} %param.12), kind=kOutput, calls=%fused_computation.17 | convolution fusion | flops 1880883200 | bytes 13369344 | tf_op jit(solution)/shard_map/dot_general | solution.py:44
  122.4 0.0 reduce-scatter.2.cloned.1.call-update
  122.5 5.2 %fusion.10 = bf16[1,1,3584,1024]{2,3,1,0:T(8,128)(2,1)} fusion(bf16[256,1024]{1,0:T(8,128)(2,1)S(1)} %get-tuple-element.21, bf16[256,3584]{1,0:T(8,128)(2,1)S(1)} %copy-done), kind=kOutput, calls=%fused_computation.13 | convolution fusion | flops 1882718208 | bytes 9699328 | tf_op jit(solution)/shard_map/dot_general | solution.py:49
  127.6 10.4 %copy.27 = bf16[1,1,3584,1024]{3,2,1,0:T(8,128)(2,1)} copy(bf16[1,1,3584,1024]{2,3,1,0:T(8,128)(2,1)} %fusion.10) | data formatting | bytes 14680064
  138.0 5.2 %fusion.11 = bf16[1,1,3584,1024]{2,3,1,0:T(8,128)(2,1)} fusion(bf16[256,1024]{1,0:T(8,128)(2,1)S(1)} %get-tuple-element.20, bf16[256,3584]{1,0:T(8,128)(2,1)S(1)} %copy-done), kind=kOutput, calls=%fused_computation.14 | convolution fusion | flops 1882718208 | bytes 9699328 | tf_op jit(solution)/shard_map/dot_general | solution.py:50
  143.2 10.6 %copy.28 = bf16[1,1,3584,1024]{3,2,1,0:T(8,128)(2,1)} copy(bf16[1,1,3584,1024]{2,3,1,0:T(8,128)(2,1)} %fusion.11) | data formatting | bytes 14680064
  153.8 0.0 copy-done.4
  153.8 6.9 %fusion.12 = bf16[1,1,1024,3584]{3,2,1,0:T(8,128)(2,1)} fusion(bf16[256,3584]{1,0:T(8,128)(2,1)S(1)} %copy-done.4, f32[256]{0:T(256)S(1)} %bitcast.52, f32[256,1024]{1,0:T(8,128)} %fusion.6, f32[256,1024]{1,0:T(8,128)} %fusion.2), kind=kOutput, calls=%fused_computation.15 | convolution fusion | flops 1887043584 | bytes 11273216 | tf_op jit(solution)/shard_map/dot_general | solution.py:48
  160.7 27.3 %reduce-scatter.2.cloned.1.call-done = bf16[32,3584]{1,0:T(8,128)(2,1)} async-done(((bf16[256,3584]{1,0:T(8,128)(2,1)}), bf16[32,3584]{1,0:T(8,128)(2,1)}) %reduce-scatter.2.cloned.1.call-update) | async-done | bytes 229392 | tf_op jit(solution)/shard_map/reduce_scatter | solution.py:45
  188.0 0.0 copy-done.2
  188.0 1.7 add_convert_fusion
  (7 shorter events, 0.0 us)
Async XLA Ops:
  7.2 51.9 %all-gather.6.cloned.1.call-start = ((), (), s32[]{:S(2)}) async-start(), calls=%async_computation.2 | async-start | bytes 2064384 | tf_op jit(solution)/shard_map/all_gather | solution.py:25
  7.9 99.4 %all-gather.4.cloned.1.call-start = ((), (), s32[]{:S(2)}) async-start(), calls=%async_computation.1 | async-start | bytes 2064384 | tf_op jit(solution)/shard_map/all_gather | solution.py:26
  7.9 6.3 %collective-permute-start = (bf16[32,3584]{1,0:T(8,128)(2,1)}, bf16[32,3584]{1,0:T(8,128)(2,1)S(1)}, u32[]{:S(2)}, u32[]{:S(2)}) collective-permute-start(bf16[32,3584]{1,0:T(8,128)(2,1)} %bitcast.53), channel_id=1, source_target_pairs={{0,24},{8,0},{16,8},{24,16},{1,25},{9,1},{17,9},{25,17},{2,26},{10... | collective-permute-start | bytes 688136 | tf_op jit(solution)/shard_map/ppermute | solution.py:9
  14.2 0.7 copy-start.1
  14.9 173.0 %reduce-scatter.2.cloned.1.call-start = ((), (), s32[]{:S(2)}) async-start(), calls=%async_computation.3 | async-start | bytes 2064384 | tf_op jit(solution)/shard_map/reduce_scatter | solution.py:45
  59.1 6.8 %copy-start = (bf16[256,3584]{1,0:T(8,128)(2,1)S(1)}, bf16[256,3584]{1,0:T(8,128)(2,1)}, u32[]{:S(2)}) copy-start(bf16[256,3584]{1,0:T(8,128)(2,1)} %all-gather.6.cloned.1.call-done) | copy-start | bytes 5505028
  107.3 6.6 %copy-start.3 = (bf16[1,1,3584,1024]{3,2,1,0:T(8,128)(2,1)S(1)}, bf16[1,1,3584,1024]{3,2,1,0:T(8,128)(2,1)}, u32[]{:S(2)}) copy-start(bf16[1,1,3584,1024]{3,2,1,0:T(8,128)(2,1)} %param.11) | copy-start | bytes 22020100
  143.2 10.6 %copy-start.4 = (bf16[256,3584]{1,0:T(8,128)(2,1)S(1)}, bf16[256,3584]{1,0:T(8,128)(2,1)}, u32[]{:S(2)}) copy-start(bf16[256,3584]{1,0:T(8,128)(2,1)} %all-gather.4.cloned.1.call-done) | copy-start | bytes 5505028
  153.8 34.2 %copy-start.2 = (bf16[32,3584]{1,0:T(8,128)(2,1)S(1)}, bf16[32,3584]{1,0:T(8,128)(2,1)}, u32[]{:S(2)}) copy-start(bf16[32,3584]{1,0:T(8,128)(2,1)} %copy-done.1) | copy-start | bytes 688132
Sparse Core Ops, SparseCore 0:
  10.1 48.9 all-gather.5
  61.8 45.4 all-gather.3
  122.6 65.3 reduce-scatter.1

commit v2 on v1

v2 whole, which is shorter than its diff:
```python
import functools

import jax
import jax.numpy as jnp
from jax import lax
from jax.experimental import pallas as pl
from jax.experimental.pallas import tpu as pltpu
from jax.sharding import PartitionSpec as P

F32 = jnp.float32
BF16 = jnp.bfloat16
LAST = (((1,), (1,)), ((), ()))
FIRST = (((0,), (0,)), ((), ()))
VMEM_LIMIT = 60 * 1024 * 1024
CHUNKS = 2


def exchange_kernel(sizes, *refs):
    sections, replicas, experts = sizes
    (incoming, stash, weight, gate_hbm, up_hbm, down_hbm), refs = refs[:6], refs[6:]
    (own_up, hidden_ref, gate_grad_ref, up_grad_ref, x_out, s_out), refs = refs[:6], refs[6:]
    parts, refs = refs[: CHUNKS * replicas], refs[CHUNKS * replicas :]
    (xbuf, ubuf, wbuf, gate_w, up_w, down_w, gate_pre, up_pre) = refs[:8]
    (load_sem, out_sem, part_sem, shift_send, shift_recv, w_send, w_recv, zsend, dsend, recv) = refs[8:]
    groups, rows, width = xbuf.shape
    hid = gate_w.shape[1]
    tile = min(256, hid)
    tiles = hid // tile
    per_block = max(1, min(groups, 256 // rows))
    blocks = groups // per_block
    height = per_block * rows
    s, d, e = lax.axis_index("section"), lax.axis_index("dp"), lax.axis_index("expert")
    cut = (width // 128) * 17 // 28 * 128
    columns = (pl.ds(0, cut), pl.ds(cut, width - cut))

    def slot(replica, expert):
        return lax.rem(replica + replicas, replicas) * experts + jnp.clip(expert, 0, experts - 1)

    me = slot(d, e)
    loads = [
        pltpu.make_async_copy(src, dst, load_sem.at[i])
        for i, (src, dst) in enumerate(((gate_hbm, gate_w), (up_hbm, up_w), (down_hbm, down_w)))
    ]
    peers = [(j, k) for j in range(replicas) for k in range(experts) if j or k]

    def peer(j, k):
        return {"dp": lax.rem(d + j, replicas), "expert": lax.rem(e + k, experts)}

    before = {"section": lax.rem(s + sections - 1, sections)}
    after = {"section": lax.rem(s + 1, sections)}
    barrier = pltpu.get_barrier_semaphore()
    for target in [peer(j, k) for j, k in peers] + [before, after]:
        pl.semaphore_signal(barrier, inc=1, device_id=target, device_id_type=pl.DeviceIdType.MESH)
    xbuf[me] = stash[...]
    wbuf[me] = weight[...]
    pl.semaphore_wait(barrier, len(peers) + 2)

    def remote(src, dst, send, arrive, target):
        return pltpu.make_async_remote_copy(
            src_ref=src,
            dst_ref=dst,
            send_sem=send,
            recv_sem=arrive,
            device_id=target,
            device_id_type=pl.DeviceIdType.MESH,
        )

    bufs = (xbuf, ubuf)

    def along_z(a, c, block, way):
        ref = bufs[a].at[block, :, columns[c]]
        other = jnp.clip(e + 1 if way == 0 else e - 1, 0, experts - 1)
        return remote(ref, ref, zsend.at[a, c, way, block], recv.at[a, c, block], {"expert": other})

    def along_dp(a, c, expert, j):
        block = slot(d, expert)
        ref = bufs[a].at[block, :, columns[c]]
        at = jnp.clip(expert, 0, experts - 1)
        return remote(ref, ref, dsend.at[a, c, j - 1, at], recv.at[a, c, block], peer(j, 0))

    def arrived(a, c, block):
        ref = bufs[a].at[block, :, columns[c]]
        remote(ref, ref, zsend.at[a, c, 0, block], recv.at[a, c, block], peer(1, 0)).wait_recv()

    others = range(1, replicas)
    has = (e < experts - 1, e > 0)

    def both_ways(a, c, block):
        for way in range(2):
            pl.when(has[way])(lambda way=way: along_z(a, c, block, way).start())

    def first(a):
        for j in others:
            along_dp(a, 1, e, j).start()
        both_ways(a, 0, me)
        for j in others:
            along_dp(a, 0, e, j).start()
        both_ways(a, 1, me)

    def relay(a, c, replica, k, with_dp):
        for way, origin, there in ((0, e - k, e - k >= 0), (1, e + k, e + k < experts)):

            @pl.when(there)
            def _():
                block = slot(replica, origin)
                arrived(a, c, block)
                pl.when(has[way])(lambda: along_z(a, c, block, way).start())
                if with_dp:
                    for j in others:
                        along_dp(a, c, origin, j).start()

    def step(a, k):
        relay(a, 0, d, k, True)
        for j in others:
            if k == 1:
                arrived(a, 1, slot(d - j, e))
                both_ways(a, 1, slot(d - j, e))
            else:
                relay(a, 1, d - j, k - 1, False)
        relay(a, 1, d, k, False)

    def finish(a):
        for j in others:
            relay(a, 1, d - j, experts - 1, False)
            for expert in range(experts):
                arrived(a, 0, slot(d - j, expert))

    def sent(a):
        for c in range(2):
            for j in others:
                for expert in range(experts):
                    if c == 0:
                        along_dp(a, 0, expert, j).wait_send()
                if c == 1:
                    along_dp(a, 1, e, j).wait_send()
            for j in range(replicas if c == 1 else 1):
                for k in range(experts):
                    for way, origin, there in ((0, e - k, e - k >= 0), (1, e + k, e + k < experts)):

                        @pl.when(jnp.logical_and(there, has[way]))
                        def _():
                            along_z(a, c, slot(d - j, origin), way).wait_send()

    shift = remote(incoming, ubuf.at[me], shift_send.at[0], shift_recv.at[0], before)
    shift.start()
    first(0)
    weight_copies = []
    for n, (j, k) in enumerate(peers):
        copy = remote(wbuf.at[me], wbuf.at[me], w_send.at[n], w_recv.at[n], peer(j, k))
        copy.start()
        weight_copies.append(copy)
    for load in loads:
        load.start()
    shift.wait()
    own_up[...] = ubuf[me]
    first(1)
    for k in range(1, experts):
        step(0, k)
    finish(0)
    x_copy = pltpu.make_async_copy(xbuf, x_out, out_sem.at[0])
    x_copy.start()
    loads[0].wait()
    loads[1].wait()

    def forward(lo, hi):
        @pl.loop(lo, hi)
        def _(h):
            cols = pl.ds(pl.multiple_of(h * tile, tile), tile)

            @pl.loop(0, blocks)
            def _(r):
                x = xbuf[pl.ds(r * per_block, per_block)].reshape(height, width)
                gate_pre[h, r] = jnp.dot(x, gate_w[:, cols], preferred_element_type=F32)
                up_pre[h, r] = jnp.dot(x, up_w[:, cols], preferred_element_type=F32)

    for k in range(1, experts):
        step(1, k)
        lo, hi = tiles * (k - 1) // (experts - 1), tiles * k // (experts - 1)
        if hi > lo:
            forward(lo, hi)
    finish(1)
    for copy in weight_copies:
        copy.wait()
    sent(1)
    lane = lax.broadcasted_iota(jnp.int32, wbuf.shape[1:], 1)

    @pl.loop(0, groups)
    def _(g):
        own = jnp.sum(jnp.where(lane == e, wbuf[g], 0.0), axis=1, keepdims=True)
        ubuf[g] = (own * ubuf[g].astype(F32)).astype(BF16)

    s_copy = pltpu.make_async_copy(ubuf, s_out, out_sem.at[1])
    s_copy.start()
    loads[2].wait()

    @pl.loop(0, tiles)
    def _(h):
        cols = pl.ds(pl.multiple_of(h * tile, tile), tile)

        @pl.loop(0, blocks)
        def _(r):
            at = pl.ds(pl.multiple_of(r * height, height), height)
            scaled = ubuf[pl.ds(r * per_block, per_block)].reshape(height, width)
            grad = lax.dot_general(scaled, down_w[cols, :], LAST, preferred_element_type=F32)
            gate, up = gate_pre[h, r], up_pre[h, r]
            logistic = jax.nn.sigmoid(gate)
            active = gate * logistic
            hidden_ref[at, cols] = (active * up).astype(BF16)
            gate_grad_ref[at, cols] = (
                grad * up * logistic * (1.0 + gate * (1.0 - logistic))
            ).astype(BF16)
            up_grad_ref[at, cols] = (grad * active).astype(BF16)

    sent(0)
    x_copy.wait()
    piece = width // CHUNKS
    sub = 256
    copies = []
    for c in range(CHUNKS):

        @pl.loop(0, piece // sub)
        def _(t):
            cols = pl.ds(pl.multiple_of(c * piece + t * sub, sub), sub)

            @pl.loop(0, blocks)
            def _(r):
                at = pl.ds(pl.multiple_of(r * height, height), height)
                back = lax.dot_general(
                    gate_grad_ref[at, :], gate_w[cols, :], LAST, preferred_element_type=F32
                ) + lax.dot_general(
                    up_grad_ref[at, :], up_w[cols, :], LAST, preferred_element_type=F32
                )
                xbuf[pl.ds(r * per_block, per_block), :, cols] = back.astype(BF16).reshape(
                    per_block, rows, sub
                )

        for j in range(replicas):
            for k in range(experts):
                copy = pltpu.make_async_copy(
                    xbuf.at[slot(d + j, lax.rem(e + k, experts)), :, pl.ds(c * piece, piece)],
                    parts[c * replicas + j].at[k],
                    part_sem.at[c, j, k],
                )
                copy.start()
                copies.append(copy)
    for copy in copies:
        copy.wait()
    s_copy.wait()


def exchange(sizes, incoming, stash, weight, gate, up, down):
    _, replicas, experts = sizes
    groups = replicas * experts
    rows, width = stash.shape
    hid = gate.shape[1]
    total = groups * rows
    tile = min(256, hid)
    per_block = max(1, min(groups, 256 // rows))
    dma = pltpu.SemaphoreType.DMA
    vmem, anywhere = pl.BlockSpec(memory_space=pltpu.VMEM), pl.BlockSpec(memory_space=pl.ANY)
    shape = jax.ShapeDtypeStruct
    pre = pltpu.VMEM((hid // tile, groups // per_block, per_block * rows, tile), F32)
    tokens = pltpu.VMEM((groups, rows, width), BF16)
    return pl.pallas_call(
        functools.partial(exchange_kernel, sizes),
        out_shape=[shape((rows, width), BF16)]
        + [shape((total, hid), BF16)] * 3
        + [shape((groups, rows, width), BF16)] * 2
        + [shape((experts, rows, width // CHUNKS), BF16)] * (CHUNKS * replicas),
        in_specs=[vmem] * 3 + [anywhere] * 3,
        out_specs=[vmem] * 4 + [anywhere] * (2 + CHUNKS * replicas),
        scratch_shapes=[
            tokens,
            tokens,
            pltpu.VMEM((groups, rows, 128), F32),
            pltpu.VMEM(gate.shape, BF16),
            pltpu.VMEM(up.shape, BF16),
            pltpu.VMEM(down.shape, BF16),
            pre,
            pre,
            dma((3,)),
            dma((2,)),
            dma((CHUNKS, replicas, experts)),
            dma((1,)),
            dma((1,)),
            dma((groups - 1,)),
            dma((groups - 1,)),
            dma((2, 2, 2, groups)),
            dma((2, 2, max(1, replicas - 1), experts)),
            dma((2, 2, groups)),
        ],
        compiler_params=pltpu.CompilerParams(
            collective_id=0, has_side_effects=True, vmem_limit_bytes=VMEM_LIMIT
        ),
        cost_estimate=pl.CostEstimate(
            flops=10 * total * width * hid, bytes_accessed=6 * width * hid, transcendentals=0
        ),
    )(incoming, stash, weight, gate, up, down)


def outer_kernel(lhs, *refs):
    half = len(refs) // 2
    for rhs, out in zip(refs[:half], refs[half:]):
        out[...] = lax.dot_general(lhs[...], rhs[...], FIRST, preferred_element_type=F32).astype(
            BF16
        )


def outer(lhs, tile, *rhs):
    total, height = lhs.shape
    out_width = rhs[0].shape[1]
    tile = min(tile, height)
    return pl.pallas_call(
        outer_kernel,
        grid=(height // tile,),
        in_specs=[pl.BlockSpec((total, tile), lambda i: (0, i))]
        + [pl.BlockSpec((total, out_width), lambda i: (0, 0))] * len(rhs),
        out_specs=[pl.BlockSpec((tile, out_width), lambda i: (i, 0))] * len(rhs),
        out_shape=[jax.ShapeDtypeStruct((height, out_width), BF16)] * len(rhs),
        compiler_params=pltpu.CompilerParams(vmem_limit_bytes=50 * 1024 * 1024),
        cost_estimate=pl.CostEstimate(
            flops=2 * total * height * out_width * len(rhs),
            bytes_accessed=2 * len(rhs) * height * out_width,
            transcendentals=0,
        ),
    )(lhs, *rhs)


def passed_along(x, axis, by):
    length = lax.axis_size(axis)
    return lax.ppermute(x, axis, [(i, (i + by) % length) for i in range(length)])


def per_device(sizes, incoming, stash, expert_ids, route_weight, w_gate, w_up, w_down):
    _, replicas, experts = sizes
    mbatch, tok_rows, width = stash.shape[1:]
    rows = mbatch * tok_rows
    named = expert_ids[0][..., None] == jnp.arange(128, dtype=jnp.int32)
    weight = jnp.sum(jnp.where(named, route_weight[0][..., None], 0.0), axis=2).reshape(rows, 128)
    outs = exchange(
        sizes,
        incoming[0].reshape(rows, width),
        stash[0].reshape(rows, width),
        weight,
        w_gate[0, 0],
        w_up[0, 0],
        w_down[0, 0],
    )
    upstream, hidden, gate_grad, up_grad, tokens, scaled = outs[:6]
    parts = outs[6:]
    tokens = tokens.reshape(-1, width)
    scaled = scaled.reshape(-1, width)
    summed = []
    for c in range(CHUNKS):
        mine = parts[c * replicas : (c + 1) * replicas]
        total = mine[0].astype(F32)
        for j in range(1, replicas):
            total = total + passed_along(mine[j], "dp", j).astype(F32)
        total = total.astype(BF16)
        back = total[0].astype(F32)
        for k in range(1, experts):
            back = back + passed_along(total[k], "expert", k).astype(F32)
        summed.append(back)
    grad_gate, grad_up = outer(tokens, 512, gate_grad, up_grad)
    (grad_down,) = outer(hidden, 256, scaled)
    input_grad = (upstream.astype(F32) + jnp.concatenate(summed, axis=1)).astype(BF16)
    return (
        input_grad.reshape(1, mbatch, tok_rows, width),
        grad_gate[None, None],
        grad_up[None, None],
        grad_down[None, None],
    )


def solution(mesh):
    sizes = tuple(mesh.shape[name] for name in ("section", "dp", "expert"))
    tokens = P("section", None, ("dp", "expert"), None)
    columns = P("section", "expert", None, "dp")
    rows = P("section", "expert", "dp", None)
    return jax.shard_map(
        functools.partial(per_device, sizes),
        mesh=mesh,
        in_specs=(tokens, tokens, tokens, tokens, columns, columns, rows),
        out_specs=(tokens, columns, columns, rows),
        check_vma=False,
    )
```

time: 197 us -> 106 us (0.54)
  Pallas kernels: 0 us -> 77.2 us
  waiting for transfers between devices: 82.8 us -> 13.4 us
  matrix products: 45.5 us -> 0 us
  blocking collectives: 27.3 us -> 0 us
  local copies, waits for them, and re-layouts: 21.9 us -> 2.61 us
  between operations: 13.8 us -> 0.74 us
  starting transfers between devices: 2.55 us -> 9.79 us
    pallas_call x0 -> x3, Pallas kernels: none -> 77.2 us  [the longest x1 65.5 us: exchange(): pl.pallas_call(functools.partial(exchange_kernel, sizes), out_shape=[shap...]
    all_gather x2 -> x0, waiting for transfers between devices: 50.9 us -> none  [the longest x1 35.1 us: per_device(): ups = lax.all_gather(upstream, group, axis=0, tiled=True)]
    dot_general x8 -> x0, matrix products: 45.5 us -> none  [the longest x1 6.95 us: per_device(): lax.dot_general(hidden, scaled, contract_rows, preferred_element_type=f32)]
    all_gather x1 -> x0, blocking collectives: 27.3 us -> none  [per_device(): all_weight = lax.all_gather(token_weight, group, axis=0, tiled=True)]
    reduce_scatter x1 -> x0, waiting for transfers between devices: 27.3 us -> none  [per_device(): lax.psum_scatter(back.astype(jnp.bfloat16), group, scatter_dimension=0, t...]
    unnamed x14 -> x16, local copies, waits for them, and re-layouts: 21.8 us -> 2.56 us
    ppermute x1 -> x8, waiting for transfers between devices: 3.86 us -> 13.4 us  [passed_along(): lax.ppermute(x, axis, [(i, (i + by) % length) for i in range(length)])]
    ppermute x1 -> x8, starting transfers between devices: 2.43 us -> 9.79 us  [passed_along(): lax.ppermute(x, axis, [(i, (i + by) % length) for i in range(length)])]
  transfers between devices with their start and end apart: 4 -> 8, of which waited for: 4 -> 3; matrix products, arithmetic and copies ran while one was open for 27% -> 0% of each run, Pallas kernels for 0% -> 11%
where the time goes in v2:
time: 106 us
  Pallas kernels  77.2 us (73%)
  waiting for transfers between devices  13.4 us (13%)
  starting transfers between devices  9.79 us (9%)
  local copies, waits for them, and re-layouts  2.61 us (2%)
  other arithmetic  2.46 us (2%)
    pallas_call x1, Pallas kernels, exchange(): pl.pallas_call(functools.partial(exchange_kernel, sizes), out_shape=[shap...  65.5 us
    ppermute x8, waiting for transfers between devices, passed_along(): lax.ppermute(x, axis, [(i, (i + by) % length) for i in range(length)])  13.4 us
    pallas_call x2, Pallas kernels, outer(): pl.pallas_call(outer_kernel, grid=(height // tile,), in_specs=[pl.BlockSp...  11.7 us
    ppermute x8, starting transfers between devices, passed_along(): lax.ppermute(x, axis, [(i, (i + by) % length) for i in range(length)])  9.79 us
    unnamed x16, local copies, waits for them, and re-layouts  2.56 us
  transfers between devices with their start and end apart: 8, of which 3 were waited for; matrix products, arithmetic and copies ran while one was open for 0% of the time, Pallas kernels for 11%

profile of v2, /device:TPU:0, one launch (start us, length us, event | category | flops | bytes accessed | tf_op | source)
XLA Modules:
  0.0 106.1 jit_solution(3528312116890386852)
XLA Ops:
  0.6 1.4 %select_reduce_fusion = f32[2,16,128]{2,1,0:T(8,128)} fusion(f32[2,16,2]{1,2,0:T(2,128)} %bitcast.41, s32[2,16,2]{1,2,0:T(2,128)} %bitcast.42), kind=kLoop, calls=%fused_computation.18 | loop fusion | flops 20480 | bytes 16896 | tf_op jit(solution)/shard_map/reduce_sum | solution.py:339
  2.0 65.5 %shard_map.102 = (bf16[32,3584]{1,0:T(8,128)(2,1)}, bf16[256,1024]{1,0:T(8,128)(2,1)}, bf16[256,1024]{1,0:T(8,128)(2,1)}, bf16[256,1024]{1,0:T(8,128)(2,1)}, bf1...) custom-call(bf16[32,3584]{1,0:T(8,128)(2,1)} %bitcast.46, ...), custom_call_target="tpu_custom_call" | custom-call | flops 9395240960 | bytes 22020096 | tf_op jit(solution)/shard_map/pallas_call | solution.py:264
  67.5 0.7 collective-permute-start
  68.2 1.4 %collective-permute-start.4 = (bf16[4,32,1792]{2,1,0:T(8,128)(2,1)}, bf16[4,32,1792]{2,1,0:T(8,128)(2,1)S(1)}, u32[]{:S(2)}, u32[]{:S(2)}) collective-permute-start(bf16[4,32,1792]{2,1,0:T(8,128)(2,1)} %get-tuple-element.20), channel_id=1, source_target_pairs={{0,4},{4,0},{1,5},{5,1},{2,6},{6,2},{3,7},{7,3},{8,12},{12,8},{9,1... | collective-permute-start | bytes 1376264 | tf_op jit(solution)/shard_map/ppermute | solution.py:331
  69.6 1.5 %copy-done = bf16[8,32,3584]{2,1,0:T(8,128)(2,1)S(1)} copy-done((bf16[8,32,3584]{2,1,0:T(8,128)(2,1)S(1)}, bf16[8,32,3584]{2,1,0:T(8,128)(2,1)}, u32[]{:S(2)}) %copy-start) | copy-done | bytes 1835032
  71.1 1.0 copy-done.1
  72.2 4.5 %shard_map.104 = bf16[1024,3584]{1,0:T(8,128)(2,1)} custom-call(bf16[256,1024]{1,0:T(8,128)(2,1)S(1)} %copy-done.1, bf16[256,3584]{1,0:T(8,128)(2,1)S(1)} %bitcast.36), custom_call_target="tpu_custom_call" | custom-call | flops 1879048192 | bytes 7340032 | tf_op jit(solution)/shard_map/pallas_call | solution.py:313
  76.7 0.0 copy-done.2
  76.7 0.0 copy-done.3
  76.7 0.0 copy-done.4
  76.7 0.0 copy-start.5
  76.7 0.0 copy-start.7
  76.7 7.1 %shard_map.103 = (bf16[3584,1024]{1,0:T(8,128)(2,1)}, bf16[3584,1024]{1,0:T(8,128)(2,1)}) custom-call(bf16[256,3584]{1,0:T(8,128)(2,1)S(1)} %bitcast.37, bf16[256,1024]{1,0:T(8,128)(2,1)S(1)} %copy-done.3, bf16[256,1024]{1,0:T(8,128)(2,1)S(1)} %copy-done.4), custom_call_target="tpu_custom_call" | custom-call | flops 3758096384 | bytes 14680064 | tf_op jit(solution)/shard_map/pallas_call | solution.py:313
  83.9 0.0 collective-permute-done
  83.9 0.1 add_convert_fusion.1
  84.0 0.1 collective-permute-start.1
  84.1 2.4 %collective-permute-start.2 = (bf16[32,1792]{1,0:T(8,128)(2,1)S(1)}, bf16[32,1792]{1,0:T(8,128)(2,1)S(1)}, u32[]{:S(2)}, u32[]{:S(2)}) collective-permute-start(bf16[32,1792]{1,0:T(8,128)(2,1)S(1)} %get-tuple-element.30), channel_id=1, source_target_pairs={{0,2},{1,3},{2,0},{3,1},{4,6},{5,7},{6,4},{7,5},{8,10},{9,11},{10,... | collective-permute-start | bytes 344072 | tf_op jit(solution)/shard_map/ppermute | solution.py:331
  86.5 1.4 %collective-permute-start.3 = (bf16[32,1792]{1,0:T(8,128)(2,1)S(1)}, bf16[32,1792]{1,0:T(8,128)(2,1)S(1)}, u32[]{:S(2)}, u32[]{:S(2)}) collective-permute-start(bf16[32,1792]{1,0:T(8,128)(2,1)S(1)} %get-tuple-element.29), channel_id=1, source_target_pairs={{0,3},{1,0},{2,1},{3,2},{4,7},{5,4},{6,5},{7,6},{8,11},{9,8},{10,9... | collective-permute-start | bytes 344072 | tf_op jit(solution)/shard_map/ppermute | solution.py:331
  87.9 2.2 %collective-permute-done.4 = bf16[4,32,1792]{2,1,0:T(8,128)(2,1)S(1)} collective-permute-done((bf16[4,32,1792]{2,1,0:T(8,128)(2,1)}, bf16[4,32,1792]{2,1,0:T(8,128)(2,1)S(1)}, u32[]{:S(2)}, u32[]{:S(2)}) %collective-permute-start.4) | collective-permute-done | bytes 458784 | tf_op jit(solution)/shard_map/ppermute | solution.py:331
  90.1 0.1 add_convert_fusion
  90.3 0.1 collective-permute-start.5
  90.4 1.6 %collective-permute-start.6 = (bf16[32,1792]{1,0:T(8,128)(2,1)S(1)}, bf16[32,1792]{1,0:T(8,128)(2,1)S(1)}, u32[]{:S(2)}, u32[]{:S(2)}) collective-permute-start(bf16[32,1792]{1,0:T(8,128)(2,1)S(1)} %get-tuple-element.33), channel_id=1, source_target_pairs={{0,2},{1,3},{2,0},{3,1},{4,6},{5,7},{6,4},{7,5},{8,10},{9,11},{10,... | collective-permute-start | bytes 344072 | tf_op jit(solution)/shard_map/ppermute | solution.py:331
  91.9 0.1 collective-permute-done.1
  92.0 2.2 %collective-permute-start.7 = (bf16[32,1792]{1,0:T(8,128)(2,1)S(1)}, bf16[32,1792]{1,0:T(8,128)(2,1)S(1)}, u32[]{:S(2)}, u32[]{:S(2)}) collective-permute-start(bf16[32,1792]{1,0:T(8,128)(2,1)S(1)} %get-tuple-element.32), channel_id=1, source_target_pairs={{0,3},{1,0},{2,1},{3,2},{4,7},{5,4},{6,5},{7,6},{8,11},{9,8},{10,9... | collective-permute-start | bytes 344072 | tf_op jit(solution)/shard_map/ppermute | solution.py:331
  94.2 5.0 %collective-permute-done.2 = bf16[32,1792]{1,0:T(8,128)(2,1)S(1)} collective-permute-done((bf16[32,1792]{1,0:T(8,128)(2,1)S(1)}, bf16[32,1792]{1,0:T(8,128)(2,1)S(1)}, u32[]{:S(2)}, u32[]{:S(2)}) %collective-permute-start.2) | collective-permute-done | bytes 114720 | tf_op jit(solution)/shard_map/ppermute | solution.py:331
  99.2 0.0 collective-permute-done.3
  99.2 0.1 fusion.4
  99.2 0.0 collective-permute-done.5
  99.2 6.1 %collective-permute-done.6 = bf16[32,1792]{1,0:T(8,128)(2,1)S(1)} collective-permute-done((bf16[32,1792]{1,0:T(8,128)(2,1)S(1)}, bf16[32,1792]{1,0:T(8,128)(2,1)S(1)}, u32[]{:S(2)}, u32[]{:S(2)}) %collective-permute-start.6) | collective-permute-done | bytes 114720 | tf_op jit(solution)/shard_map/ppermute | solution.py:331
  105.3 0.0 collective-permute-done.7
  105.3 0.1 fusion.2
  105.4 0.7 fusion
  (11 shorter events, 0.1 us)
Async XLA Ops:
  67.5 16.3 %collective-permute-start = (bf16[4,32,1792]{2,1,0:T(8,128)(2,1)}, bf16[4,32,1792]{2,1,0:T(8,128)(2,1)S(1)}, u32[]{:S(2)}, u32[]{:S(2)}) collective-permute-start(bf16[4,32,1792]{2,1,0:T(8,128)(2,1)} %get-tuple-element.18), channel_id=1, source_target_pairs={{0,4},{4,0},{1,5},{5,1},{2,6},{6,2},{3,7},{7,3},{8,12},{12,8},{9,1... | collective-permute-start | bytes 1376264 | tf_op jit(solution)/shard_map/ppermute | solution.py:331
  68.2 21.9 %collective-permute-start.4 = (bf16[4,32,1792]{2,1,0:T(8,128)(2,1)}, bf16[4,32,1792]{2,1,0:T(8,128)(2,1)S(1)}, u32[]{:S(2)}, u32[]{:S(2)}) collective-permute-start(bf16[4,32,1792]{2,1,0:T(8,128)(2,1)} %get-tuple-element.20), channel_id=1, source_target_pairs={{0,4},{4,0},{1,5},{5,1},{2,6},{6,2},{3,7},{7,3},{8,12},{12,8},{9,1... | collective-permute-start | bytes 1376264 | tf_op jit(solution)/shard_map/ppermute | solution.py:331
  69.6 1.5 %copy-start = (bf16[8,32,3584]{2,1,0:T(8,128)(2,1)S(1)}, bf16[8,32,3584]{2,1,0:T(8,128)(2,1)}, u32[]{:S(2)}) copy-start(bf16[8,32,3584]{2,1,0:T(8,128)(2,1)} %get-tuple-element.27) | copy-start | bytes 5505028
  71.1 1.0 copy-start.1
  72.2 4.5 %copy-start.2 = (bf16[8,32,3584]{2,1,0:T(8,128)(2,1)S(1)}, bf16[8,32,3584]{2,1,0:T(8,128)(2,1)}, u32[]{:S(2)}) copy-start(bf16[8,32,3584]{2,1,0:T(8,128)(2,1)} %get-tuple-element.21) | copy-start | bytes 5505028
  72.2 4.5 %copy-start.3 = (bf16[256,1024]{1,0:T(8,128)(2,1)S(1)}, bf16[256,1024]{1,0:T(8,128)(2,1)}, u32[]{:S(2)}) copy-start(bf16[256,1024]{1,0:T(8,128)(2,1)} %get-tuple-element.22.refs_0_) | copy-start | bytes 1572868
  72.2 4.5 %copy-start.4 = (bf16[256,1024]{1,0:T(8,128)(2,1)S(1)}, bf16[256,1024]{1,0:T(8,128)(2,1)}, u32[]{:S(2)}) copy-start(bf16[256,1024]{1,0:T(8,128)(2,1)} %get-tuple-element.23.refs_1_) | copy-start | bytes 1572868
  76.7 7.2 %copy-start.6 = (bf16[4,32,1792]{2,1,0:T(8,128)(2,1)S(1)}, bf16[4,32,1792]{2,1,0:T(8,128)(2,1)}, u32[]{:S(2)}) copy-start(bf16[4,32,1792]{2,1,0:T(8,128)(2,1)} %get-tuple-element.17) | copy-start | bytes 1376260
  76.7 13.4 %copy-start.5 = (bf16[4,32,1792]{2,1,0:T(8,128)(2,1)S(1)}, bf16[4,32,1792]{2,1,0:T(8,128)(2,1)}, u32[]{:S(2)}) copy-start(bf16[4,32,1792]{2,1,0:T(8,128)(2,1)} %get-tuple-element.19) | copy-start | bytes 1376260
  76.7 28.7 %copy-start.7 = (bf16[32,3584]{1,0:T(8,128)(2,1)S(1)}, bf16[32,3584]{1,0:T(8,128)(2,1)}, u32[]{:S(2)}) copy-start(bf16[32,3584]{1,0:T(8,128)(2,1)} %get-tuple-element.16) | copy-start | bytes 688132
  84.0 8.0 %collective-permute-start.1 = (bf16[32,1792]{1,0:T(8,128)(2,1)S(1)}, bf16[32,1792]{1,0:T(8,128)(2,1)S(1)}, u32[]{:S(2)}, u32[]{:S(2)}) collective-permute-start(bf16[32,1792]{1,0:T(8,128)(2,1)S(1)} %get-tuple-element.28), channel_id=1, source_target_pairs={{0,1},{1,2},{2,3},{3,0},{4,5},{5,6},{6,7},{7,4},{8,9},{9,10},{10,1... | collective-permute-start | bytes 344072 | tf_op jit(solution)/shard_map/ppermute | solution.py:331
  84.1 15.1 %collective-permute-start.2 = (bf16[32,1792]{1,0:T(8,128)(2,1)S(1)}, bf16[32,1792]{1,0:T(8,128)(2,1)S(1)}, u32[]{:S(2)}, u32[]{:S(2)}) collective-permute-start(bf16[32,1792]{1,0:T(8,128)(2,1)S(1)} %get-tuple-element.30), channel_id=1, source_target_pairs={{0,2},{1,3},{2,0},{3,1},{4,6},{5,7},{6,4},{7,5},{8,10},{9,11},{10,... | collective-permute-start | bytes 344072 | tf_op jit(solution)/shard_map/ppermute | solution.py:331
  86.5 12.7 %collective-permute-start.3 = (bf16[32,1792]{1,0:T(8,128)(2,1)S(1)}, bf16[32,1792]{1,0:T(8,128)(2,1)S(1)}, u32[]{:S(2)}, u32[]{:S(2)}) collective-permute-start(bf16[32,1792]{1,0:T(8,128)(2,1)S(1)} %get-tuple-element.29), channel_id=1, source_target_pairs={{0,3},{1,0},{2,1},{3,2},{4,7},{5,4},{6,5},{7,6},{8,11},{9,8},{10,9... | collective-permute-start | bytes 344072 | tf_op jit(solution)/shard_map/ppermute | solution.py:331
  90.3 8.9 %collective-permute-start.5 = (bf16[32,1792]{1,0:T(8,128)(2,1)S(1)}, bf16[32,1792]{1,0:T(8,128)(2,1)S(1)}, u32[]{:S(2)}, u32[]{:S(2)}) collective-permute-start(bf16[32,1792]{1,0:T(8,128)(2,1)S(1)} %get-tuple-element.31), channel_id=1, source_target_pairs={{0,1},{1,2},{2,3},{3,0},{4,5},{5,6},{6,7},{7,4},{8,9},{9,10},{10,1... | collective-permute-start | bytes 344072 | tf_op jit(solution)/shard_map/ppermute | solution.py:331
  90.4 15.0 %collective-permute-start.6 = (bf16[32,1792]{1,0:T(8,128)(2,1)S(1)}, bf16[32,1792]{1,0:T(8,128)(2,1)S(1)}, u32[]{:S(2)}, u32[]{:S(2)}) collective-permute-start(bf16[32,1792]{1,0:T(8,128)(2,1)S(1)} %get-tuple-element.33), channel_id=1, source_target_pairs={{0,2},{1,3},{2,0},{3,1},{4,6},{5,7},{6,4},{7,5},{8,10},{9,11},{10,... | collective-permute-start | bytes 344072 | tf_op jit(solution)/shard_map/ppermute | solution.py:331
  92.0 13.3 %collective-permute-start.7 = (bf16[32,1792]{1,0:T(8,128)(2,1)S(1)}, bf16[32,1792]{1,0:T(8,128)(2,1)S(1)}, u32[]{:S(2)}, u32[]{:S(2)}) collective-permute-start(bf16[32,1792]{1,0:T(8,128)(2,1)S(1)} %get-tuple-element.32), channel_id=1, source_target_pairs={{0,3},{1,0},{2,1},{3,2},{4,7},{5,4},{6,5},{7,6},{8,11},{9,8},{10,9... | collective-permute-start | bytes 344072 | tf_op jit(solution)/shard_map/ppermute | solution.py:331

commit v3 on v2

--- a/solution.py
+++ b/solution.py
@@ -12,16 +12,16 @@
 LAST = (((1,), (1,)), ((), ()))
 FIRST = (((0,), (0,)), ((), ()))
 VMEM_LIMIT = 60 * 1024 * 1024
-CHUNKS = 2
+CHUNKS = 7
 
 
 def exchange_kernel(sizes, *refs):
     sections, replicas, experts = sizes
     (incoming, stash, weight, gate_hbm, up_hbm, down_hbm), refs = refs[:6], refs[6:]
     (own_up, hidden_ref, gate_grad_ref, up_grad_ref, x_out, s_out), refs = refs[:6], refs[6:]
-    parts, refs = refs[: CHUNKS * replicas], refs[CHUNKS * replicas :]
-    (xbuf, ubuf, wbuf, gate_w, up_w, down_w, gate_pre, up_pre) = refs[:8]
-    (load_sem, out_sem, part_sem, shift_send, shift_recv, w_send, w_recv, zsend, dsend, recv) = refs[8:]
+    (xbuf, ubuf, wbuf, back_buf, gate_w, up_w, down_w, gate_pre, up_pre) = refs[:9]
+    (load_sem, out_sem, shift_send, shift_recv, w_send, w_recv, zsend, dsend, recv) = refs[9:18]
+    (ready, y_send, y_recv, z_send, z_recv) = refs[18:]
     groups, rows, width = xbuf.shape
     hid = gate_w.shape[1]
     tile = min(256, hid)
@@ -213,14 +213,37 @@
 
     sent(0)
     x_copy.wait()
+    s_copy.wait()
+    for j in others:
+        pl.semaphore_signal(
+            ready, inc=1, device_id=peer(j, 0), device_id_type=pl.DeviceIdType.MESH
+        )
     piece = width // CHUNKS
-    sub = 256
-    copies = []
-    for c in range(CHUNKS):
-
-        @pl.loop(0, piece // sub)
-        def _(t):
-            cols = pl.ds(pl.multiple_of(c * piece + t * sub, sub), sub)
+
+    def to_replica(c, j):
+        cols = pl.ds(c * piece, piece)
+        theirs = pl.ds(lax.rem(d + j, replicas) * experts, experts)
+        return remote(
+            xbuf.at[theirs, :, cols],
+            ubuf.at[pl.ds(j * experts, experts), :, cols],
+            y_send.at[c, j - 1],
+            y_recv.at[c, j - 1],
+            peer(j, 0),
+        )
+
+    def to_expert(c, k):
+        cols = pl.ds(c * piece, piece)
+        return remote(
+            xbuf.at[slot(d, lax.rem(e + k, experts)), :, cols],
+            back_buf.at[k - 1, :, cols],
+            z_send.at[c, k - 1],
+            z_recv.at[c, k - 1],
+            peer(0, k),
+        )
+
+    for c in range(CHUNKS + 2):
+        if c < CHUNKS:
+            cols = pl.ds(c * piece, piece)
 
             @pl.loop(0, blocks)
             def _(r):
@@ -231,21 +254,36 @@
                     up_grad_ref[at, :], up_w[cols, :], LAST, preferred_element_type=F32
                 )
                 xbuf[pl.ds(r * per_block, per_block), :, cols] = back.astype(BF16).reshape(
-                    per_block, rows, sub
+                    per_block, rows, piece
                 )
 
-        for j in range(replicas):
-            for k in range(experts):
-                copy = pltpu.make_async_copy(
-                    xbuf.at[slot(d + j, lax.rem(e + k, experts)), :, pl.ds(c * piece, piece)],
-                    parts[c * replicas + j].at[k],
-                    part_sem.at[c, j, k],
-                )
-                copy.start()
-                copies.append(copy)
-    for copy in copies:
-        copy.wait()
-    s_copy.wait()
+            if c == 0 and replicas > 1:
+                pl.semaphore_wait(ready, replicas - 1)
+            for j in others:
+                to_replica(c, j).start()
+        if c >= 2:
+            q = c - 2
+            cols = pl.ds(q * piece, piece)
+            own = pl.ds(d * experts, experts)
+            total = xbuf[own, :, cols].astype(F32)
+            for j in others:
+                to_replica(q, j).wait_recv()
+                total = total + ubuf[pl.ds(j * experts, experts), :, cols].astype(F32)
+            xbuf[own, :, cols] = total.astype(BF16)
+            for k in range(1, experts):
+                to_expert(q, k).start()
+    for c in range(CHUNKS):
+        cols = pl.ds(c * piece, piece)
+        back = xbuf[me, :, cols].astype(F32)
+        for k in range(1, experts):
+            to_expert(c, k).wait_recv()
+            back = back + back_buf[k - 1, :, cols].astype(F32)
+        own_up[:, cols] = (own_up[:, cols].astype(F32) + back).astype(BF16)
+    for c in range(CHUNKS):
+        for j in others:
+            to_replica(c, j).wait_send()
+        for k in range(1, experts):
+            to_expert(c, k).wait_send()
 
 
 def exchange(sizes, incoming, stash, weight, gate, up, down):
@@ -265,14 +303,14 @@
         functools.partial(exchange_kernel, sizes),
         out_shape=[shape((rows, width), BF16)]
         + [shape((total, hid), BF16)] * 3
-        + [shape((groups, rows, width), BF16)] * 2
-        + [shape((experts, rows, width // CHUNKS), BF16)] * (CHUNKS * replicas),
+        + [shape((groups, rows, width), BF16)] * 2,
         in_specs=[vmem] * 3 + [anywhere] * 3,
-        out_specs=[vmem] * 4 + [anywhere] * (2 + CHUNKS * replicas),
+        out_specs=[vmem] * 4 + [anywhere] * 2,
         scratch_shapes=[
             tokens,
             tokens,
             pltpu.VMEM((groups, rows, 128), F32),
+            pltpu.VMEM((max(1, experts - 1), rows, width), BF16),
             pltpu.VMEM(gate.shape, BF16),
             pltpu.VMEM(up.shape, BF16),
             pltpu.VMEM(down.shape, BF16),
@@ -280,7 +318,6 @@
             pre,
             dma((3,)),
             dma((2,)),
-            dma((CHUNKS, replicas, experts)),
             dma((1,)),
             dma((1,)),
             dma((groups - 1,)),
@@ -288,6 +325,11 @@
             dma((2, 2, 2, groups)),
             dma((2, 2, max(1, replicas - 1), experts)),
             dma((2, 2, groups)),
+            pltpu.SemaphoreType.REGULAR,
+            dma((CHUNKS, max(1, replicas - 1))),
+            dma((CHUNKS, max(1, replicas - 1))),
+            dma((CHUNKS, max(1, experts - 1))),
+            dma((CHUNKS, max(1, experts - 1))),
         ],
         compiler_params=pltpu.CompilerParams(
             collective_id=0, has_side_effects=True, vmem_limit_bytes=VMEM_LIMIT
@@ -317,7 +359,7 @@
         + [pl.BlockSpec((total, out_width), lambda i: (0, 0))] * len(rhs),
         out_specs=[pl.BlockSpec((tile, out_width), lambda i: (i, 0))] * len(rhs),
         out_shape=[jax.ShapeDtypeStruct((height, out_width), BF16)] * len(rhs),
-        compiler_params=pltpu.CompilerParams(vmem_limit_bytes=50 * 1024 * 1024),
+        compiler_params=pltpu.CompilerParams(vmem_limit_bytes=VMEM_LIMIT),
         cost_estimate=pl.CostEstimate(
             flops=2 * total * height * out_width * len(rhs),
             bytes_accessed=2 * len(rhs) * height * out_width,
@@ -326,13 +368,7 @@
     )(lhs, *rhs)
 
 
-def passed_along(x, axis, by):
-    length = lax.axis_size(axis)
-    return lax.ppermute(x, axis, [(i, (i + by) % length) for i in range(length)])
-
-
 def per_device(sizes, incoming, stash, expert_ids, route_weight, w_gate, w_up, w_down):
-    _, replicas, experts = sizes
     mbatch, tok_rows, width = stash.shape[1:]
     rows = mbatch * tok_rows
     named = expert_ids[0][..., None] == jnp.arange(128, dtype=jnp.int32)
@@ -346,24 +382,11 @@
         w_up[0, 0],
         w_down[0, 0],
     )
-    upstream, hidden, gate_grad, up_grad, tokens, scaled = outs[:6]
-    parts = outs[6:]
+    input_grad, hidden, gate_grad, up_grad, tokens, scaled = outs
     tokens = tokens.reshape(-1, width)
     scaled = scaled.reshape(-1, width)
-    summed = []
-    for c in range(CHUNKS):
-        mine = parts[c * replicas : (c + 1) * replicas]
-        total = mine[0].astype(F32)
-        for j in range(1, replicas):
-            total = total + passed_along(mine[j], "dp", j).astype(F32)
-        total = total.astype(BF16)
-        back = total[0].astype(F32)
-        for k in range(1, experts):
-            back = back + passed_along(total[k], "expert", k).astype(F32)
-        summed.append(back)
     grad_gate, grad_up = outer(tokens, 512, gate_grad, up_grad)
     (grad_down,) = outer(hidden, 256, scaled)
-    input_grad = (upstream.astype(F32) + jnp.concatenate(summed, axis=1)).astype(BF16)
     return (
         input_grad.reshape(1, mbatch, tok_rows, width),
         grad_gate[None, None],

time: 106 us -> 102 us (0.962)
  Pallas kernels: 77.2 us -> 99.2 us
  waiting for transfers between devices: 13.4 us -> 0 us
  starting transfers between devices: 9.79 us -> 0 us
  local copies, waits for them, and re-layouts: 2.61 us -> 0.69 us
  other arithmetic: 2.46 us -> 1.39 us
    pallas_call x1, Pallas kernels: 65.5 us -> 83.9 us  [exchange(): pl.pallas_call(functools.partial(exchange_kernel, sizes), out_shape=[shap...]
    ppermute x8 -> x0, waiting for transfers between devices: 13.4 us -> none  [passed_along(): lax.ppermute(x, axis, [(i, (i + by) % length) for i in range(length)])]
    ppermute x8 -> x0, starting transfers between devices: 9.79 us -> none  [passed_along(): lax.ppermute(x, axis, [(i, (i + by) % length) for i in range(length)])]
    pallas_call x2, Pallas kernels: 11.7 us -> 15.3 us  [outer(): pl.pallas_call(outer_kernel, grid=(height // tile,), in_specs=[pl.BlockSp...]
    unnamed x16 -> x3, local copies, waits for them, and re-layouts: 2.56 us -> 0.69 us
  transfers between devices with their start and end apart: 8 -> 0, of which waited for: 3 -> 0; matrix products, arithmetic and copies ran while one was open for 0% -> 0% of each run, Pallas kernels for 11% -> 0%
where the time goes in v3:
time: 102 us
  Pallas kernels  99.2 us (97%)
  other arithmetic  1.39 us (1%)
    pallas_call x1, Pallas kernels, exchange(): pl.pallas_call(functools.partial(exchange_kernel, sizes), out_shape=[shap...  83.9 us
    pallas_call x2, Pallas kernels, outer(): pl.pallas_call(outer_kernel, grid=(height // tile,), in_specs=[pl.BlockSp...  15.3 us

profile of v3, /device:TPU:0, one launch (start us, length us, event | category | flops | bytes accessed | tf_op | source)
XLA Modules:
  0.0 101.9 jit_solution(18222363852879368464)
XLA Ops:
  0.6 1.4 %select_reduce_fusion = f32[2,16,128]{2,1,0:T(8,128)} fusion(f32[2,16,2]{1,2,0:T(2,128)} %bitcast.18, s32[2,16,2]{1,2,0:T(2,128)} %bitcast.19), kind=kLoop, calls=%fused_computation | loop fusion | flops 20480 | bytes 16896 | tf_op jit(solution)/shard_map/reduce_sum | solution.py:375
  2.0 83.9 %shard_map.102 = (bf16[32,3584]{1,0:T(8,128)(2,1)}, bf16[256,1024]{1,0:T(8,128)(2,1)}, bf16[256,1024]{1,0:T(8,128)(2,1)}, bf16[256,1024]{1,0:T(8,128)(2,1)}, bf1...) custom-call(bf16[32,3584]{1,0:T(8,128)(2,1)} %bitcast.23, bf16[32,3584]{1,0:T(8,128)(2,1)} %bitcast.24, ...), custom_call_target="tpu_custom_call" | custom-call | flops 9395240960 | bytes 22020096 | tf_op jit(solution)/shard_map/pallas_call | solution.py:302
  85.9 8.9 %shard_map.103 = (bf16[3584,1024]{1,0:T(8,128)(2,1)}, bf16[3584,1024]{1,0:T(8,128)(2,1)}) custom-call(bf16[256,3584]{1,0:T(8,128)(2,1)} %bitcast.27, bf16[256,1024]{1,0:T(8,128)(2,1)} %get-tuple-element.14.refs_0_, bf16[256,1024]{1,0:T(8,128)(2,1)} %get-tuple-element.15.refs_1_), custom_call_target="tpu_custom_call" | custom-call | flops 3758096384 | bytes 14680064 | tf_op jit(solution)/shard_map/pallas_call | solution.py:355
  94.8 0.0 copy-start
  94.8 6.4 %shard_map.104 = bf16[1024,3584]{1,0:T(8,128)(2,1)} custom-call(bf16[256,1024]{1,0:T(8,128)(2,1)} %get-tuple-element.18.lhs, bf16[256,3584]{1,0:T(8,128)(2,1)} %bitcast.15), custom_call_target="tpu_custom_call" | custom-call | flops 1879048192 | bytes 7340032 | tf_op jit(solution)/shard_map/pallas_call | solution.py:355
  101.2 0.0 copy-done
  101.2 0.7 copy.14
Async XLA Ops:
  94.8 6.4 %copy-start = (bf16[32,3584]{1,0:T(8,128)(2,1)S(1)}, bf16[32,3584]{1,0:T(8,128)(2,1)}, u32[]{:S(2)}) copy-start(bf16[32,3584]{1,0:T(8,128)(2,1)} %get-tuple-element.12) | copy-start | bytes 688132

commit v4 on v3

--- a/solution.py
+++ b/solution.py
@@ -156,6 +156,8 @@
     first(1)
     for k in range(1, experts):
         step(0, k)
+        if k > 1:
+            step(1, k - 1)
     finish(0)
     x_copy = pltpu.make_async_copy(xbuf, x_out, out_sem.at[0])
     x_copy.start()
@@ -173,11 +175,10 @@
                 gate_pre[h, r] = jnp.dot(x, gate_w[:, cols], preferred_element_type=F32)
                 up_pre[h, r] = jnp.dot(x, up_w[:, cols], preferred_element_type=F32)
 
-    for k in range(1, experts):
-        step(1, k)
-        lo, hi = tiles * (k - 1) // (experts - 1), tiles * k // (experts - 1)
-        if hi > lo:
-            forward(lo, hi)
+    if tiles > 1:
+        forward(0, tiles // 2)
+    step(1, experts - 1)
+    forward(tiles // 2, tiles)
     finish(1)
     for copy in weight_copies:
         copy.wait()

time: 102 us -> 102 us (level)
  no operation moved by 1% of the time
where the time goes in v4:
time: 102 us
  Pallas kernels  99.2 us (97%)
  other arithmetic  1.39 us (1%)
    pallas_call x1, Pallas kernels, exchange(): pl.pallas_call(functools.partial(exchange_kernel, sizes), out_shape=[shap...  83.9 us
    pallas_call x2, Pallas kernels, outer(): pl.pallas_call(outer_kernel, grid=(height // tile,), in_specs=[pl.BlockSp...  15.3 us

profile of v4, /device:TPU:0, one launch (start us, length us, event | category | flops | bytes accessed | tf_op | source)
XLA Modules:
  0.0 101.9 jit_solution(15406993641223470234)
XLA Ops:
  0.6 1.4 %select_reduce_fusion = f32[2,16,128]{2,1,0:T(8,128)} fusion(f32[2,16,2]{1,2,0:T(2,128)} %bitcast.18, s32[2,16,2]{1,2,0:T(2,128)} %bitcast.19), kind=kLoop, calls=%fused_computation | loop fusion | flops 20480 | bytes 16896 | tf_op jit(solution)/shard_map/reduce_sum | solution.py:376
  2.0 83.9 %shard_map.102 = (bf16[32,3584]{1,0:T(8,128)(2,1)}, bf16[256,1024]{1,0:T(8,128)(2,1)}, bf16[256,1024]{1,0:T(8,128)(2,1)}, bf16[256,1024]{1,0:T(8,128)(2,1)}, bf1...) custom-call(bf16[32,3584]{1,0:T(8,128)(2,1)} %bitcast.23, bf16[32,3584]{1,0:T(8,128)(2,1)} %bitcast.24, ...), custom_call_target="tpu_custom_call" | custom-call | flops 9395240960 | bytes 22020096 | tf_op jit(solution)/shard_map/pallas_call | solution.py:303
  85.9 8.9 %shard_map.103 = (bf16[3584,1024]{1,0:T(8,128)(2,1)}, bf16[3584,1024]{1,0:T(8,128)(2,1)}) custom-call(bf16[256,3584]{1,0:T(8,128)(2,1)} %bitcast.27, bf16[256,1024]{1,0:T(8,128)(2,1)} %get-tuple-element.14.refs_0_, bf16[256,1024]{1,0:T(8,128)(2,1)} %get-tuple-element.15.refs_1_), custom_call_target="tpu_custom_call" | custom-call | flops 3758096384 | bytes 14680064 | tf_op jit(solution)/shard_map/pallas_call | solution.py:356
  94.8 0.0 copy-start
  94.8 6.4 %shard_map.104 = bf16[1024,3584]{1,0:T(8,128)(2,1)} custom-call(bf16[256,1024]{1,0:T(8,128)(2,1)} %get-tuple-element.18.lhs, bf16[256,3584]{1,0:T(8,128)(2,1)} %bitcast.15), custom_call_target="tpu_custom_call" | custom-call | flops 1879048192 | bytes 7340032 | tf_op jit(solution)/shard_map/pallas_call | solution.py:356
  101.2 0.0 copy-done
  101.2 0.7 copy.14
Async XLA Ops:
  94.8 6.4 %copy-start = (bf16[32,3584]{1,0:T(8,128)(2,1)S(1)}, bf16[32,3584]{1,0:T(8,128)(2,1)}, u32[]{:S(2)}) copy-start(bf16[32,3584]{1,0:T(8,128)(2,1)} %get-tuple-element.12) | copy-start | bytes 688132
